TPU v7x, 512 devices: a whole 4x8x8 slice. The times are simulated.
512 devices in a mesh: gx: 8 (over y_hi, x), gy: 8 (over y_lo, core), gz: 8 (over z).
Axes of the slice: x: 4, y: 8 (y_hi: 2, y_lo: 4; y = y_hi * 4 + y_lo), z: 8, core: 2. Of those that a mesh axis runs over, the one named last changes fastest.
Arguments:
- inputs: bfloat16 [2048, 6144], P('gx', ('gy', 'gz')), may hold values from -6 to 6
- out_grad: bfloat16 [2048, 6144], P('gx', ('gy', 'gz')), may hold values from -3 to 3
- w_in: bfloat16 [6144, 16384], P('gy', ('gx', 'gz')), may hold values from -0.078125 to 0.078125
- w_out: bfloat16 [16384, 6144], P(('gx', 'gz'), 'gy'), may hold values from -0.046875 to 0.046875
Outputs:
- input_grad: bfloat16 [2048, 6144], P('gx', ('gy', 'gz'))
- weight_grad: bfloat16 [6144, 16384], P('gy', ('gx', 'gz'))
- gram_out: float32 [8, 6144, 768], P('gz', ('gy', 'gx'))
All inputs are finite; a program needn't handle non-finite values.
Results may differ from a plain program's by a relative error of at most 0.027.
Values may be sent and summed in bfloat16 or wider, within the bound.
A program may use at most 64 MiB of HBM per device.

v0:
```python
import jax
import jax.numpy as jnp
from jax import lax
from jax.sharding import PartitionSpec as P

GELU_COEF = 0.7978845608


def gelu_slope(preact):
    inner = GELU_COEF * (preact + 0.044715 * preact * preact * preact)
    tanh_part = jnp.tanh(inner)
    return 0.5 * (1.0 + tanh_part) + 0.5 * preact * (1.0 - tanh_part * tanh_part) * GELU_COEF * (
        1.0 + 3.0 * 0.044715 * preact * preact
    )


def body(inputs, out_grad, w_in, w_out):
    x_rows, g_rows = (
        lax.all_gather(inputs, "gz", axis=1, tiled=True),
        lax.all_gather(out_grad, "gz", axis=1, tiled=True),
    )
    w_in_group = lax.all_gather(w_in, "gx", axis=1, tiled=True)
    back_part = lax.dot_general(
        g_rows,
        lax.all_gather(w_out, "gx", axis=0, tiled=True),
        (((1,), (1,)), ((), ())),
        preferred_element_type=jnp.float32,
    )
    pre_part = jnp.dot(x_rows, w_in_group, preferred_element_type=jnp.float32)
    hidden_pre, hidden_back = (
        lax.psum(pre_part.astype(jnp.bfloat16), "gy").astype(jnp.float32),
        lax.psum(back_part.astype(jnp.bfloat16), "gy").astype(jnp.float32),
    )
    hidden_grad = (hidden_back * gelu_slope(hidden_pre)).astype(jnp.bfloat16)
    dx_part = lax.dot_general(
        hidden_grad, w_in_group, (((1,), (1,)), ((), ())), preferred_element_type=jnp.float32
    )
    input_grad = lax.psum_scatter(
        dx_part.astype(jnp.bfloat16), "gz", scatter_dimension=1, tiled=True
    )
    dw_part = lax.dot_general(
        x_rows, hidden_grad, (((0,), (0,)), ((), ())), preferred_element_type=jnp.float32
    )
    weight_grad = lax.psum_scatter(
        dw_part.astype(jnp.bfloat16), "gx", scatter_dimension=1, tiled=True
    )
    grad_block = lax.all_gather(weight_grad, "gx", axis=1, tiled=True)
    block_rows = grad_block.shape[0]
    block_f32 = grad_block.astype(jnp.float32)
    block_sq = jnp.sum(block_f32 * block_f32)
    factor = 1.0 / (jnp.sqrt(block_sq) + 1e-07)
    normed = (block_f32 * factor).astype(jnp.bfloat16)
    own_count = block_rows // lax.axis_size("gx")
    own_rows = lax.dynamic_slice_in_dim(normed, lax.axis_index("gx") * own_count, own_count, 0)
    gram_rows = jnp.float32(block_rows) * lax.dot_general(
        own_rows, normed, (((1,), (1,)), ((), ())), preferred_element_type=jnp.float32
    )
    return (input_grad, weight_grad, gram_rows[None])


def solution(mesh):
    placed = (
        P("gx", ("gy", "gz")),
        P("gx", ("gy", "gz")),
        P("gy", ("gx", "gz")),
        P(("gx", "gz"), "gy"),
    )
    return jax.shard_map(
        body,
        mesh=mesh,
        in_specs=placed,
        out_specs=(P("gx", ("gy", "gz")), P("gy", ("gx", "gz")), P("gz", ("gy", "gx"), None)),
        check_vma=False,
    )
```

profile of v0, /device:TPU:1, one launch (start us, length us, event | category | flops | bytes accessed | tf_op | source)
XLA Modules:
  0.0 554.0 jit_solution(5814238299886608261)
XLA Ops:
  7.2 0.0 all-gather.4.cloned.1.call-start
  7.2 0.7 all-gather.4.cloned.1.call-update
  7.9 0.0 all-gather.6.cloned.1.call-start
  7.9 0.7 all-gather.6.cloned.1.call-update
  8.6 0.0 all-reduce.3.cloned.1.call-start
  8.7 26.4 %all_gather.17 = bf16[256,768]{0,1:T(8,128)(2,1)S(1)} all-gather(bf16[256,96]{0,1:T(8,128)(2,1)} %param.4), channel_id=1, replica_groups=mesh['gx'=8,'gy'=8,'gz'=8] {'gz'}, dimensions={1}, use_global_device_ids=true | all-gather | bytes 442368 | tf_op jit(solution)/shard_map/all_gather | solution.py:19
  35.1 21.2 %all_gather.15 = bf16[256,768]{0,1:T(8,128)(2,1)S(1)} all-gather(bf16[256,96]{0,1:T(8,128)(2,1)} %param.5), channel_id=1, replica_groups=mesh['gx'=8,'gy'=8,'gz'=8] {'gz'}, dimensions={1}, use_global_device_ids=true | all-gather | bytes 442368 | tf_op jit(solution)/shard_map/all_gather | solution.py:20
  56.3 52.9 %all-gather.4.cloned.1.call-done = bf16[2048,768]{1,0:T(8,128)(2,1)} async-done(((bf16[256,768]{1,0:T(8,128)(2,1)}), bf16[2048,768]{1,0:T(8,128)(2,1)}) %all-gather.4.cloned.1.call-update) | async-done | bytes 3145744 | tf_op jit(solution)/shard_map/all_gather | solution.py:25
  109.2 4.0 convolution_convert_fusion.2
  113.2 94.5 %all-gather.6.cloned.1.call-done = bf16[768,2048]{1,0:T(8,128)(2,1)} async-done(((bf16[768,256]{1,0:T(8,128)(2,1)}), bf16[768,2048]{1,0:T(8,128)(2,1)}) %all-gather.6.cloned.1.call-update) | async-done | bytes 3145744 | tf_op jit(solution)/shard_map/all_gather | solution.py:22
  207.7 3.9 convolution_convert_fusion.1
  211.6 0.0 reduce-scatter.5.cloned.1.call-start
  211.7 83.5 %all-reduce.3.cloned.1.call-done = (bf16[256,2048]{1,0:T(8,128)(2,1)}, bf16[256,2048]{1,0:T(8,128)(2,1)}) async-done(((bf16[256,2048]{1,0:T(8,128)(2,1)}, bf16[256,2048]{1,0:T(8,128)(2,1)}), (bf16[256,2048]{1,0:T(8,128)(2,1)}, bf16[256,2048]{1,0:T(8,128)(2,1)})) %all-reduce.3.cloned.1.call-update) | async-done | bytes 2097168 | tf_op jit(solution)/shard_map/psum | solution.py:31
  295.2 5.5 %fusion.2 = bf16[768,2048]{0,1:T(8,128)(2,1)} fusion(bf16[256,768]{0,1:T(8,128)(2,1)S(1)} %all_gather.17, bf16[256,2048]{1,0:T(8,128)(2,1)} %get-tuple-element.6, bf16[256,2048]{1,0:T(8,128)(2,1)} %get-tuple-element.7), kind=kOutput, calls=%fused_computation.12 | convolution fusion | flops 817889280 | bytes 5636096 | tf_op jit(solution)/shard_map/dot_general | solution.py:41
  300.7 0.0 all-gather.8.cloned.1.call-start
  300.8 113.6 %reduce-scatter.5.cloned.1.call-done = bf16[768,256]{0,1:T(8,128)(2,1)} async-done(((bf16[768,2048]{0,1:T(8,128)(2,1)}), bf16[768,256]{0,1:T(8,128)(2,1)}) %reduce-scatter.5.cloned.1.call-update) | async-done | bytes 393232 | tf_op jit(solution)/shard_map/reduce_scatter | solution.py:44
  414.4 0.0 reduce-scatter.3.cloned.1.call-start
  414.5 4.6 convolution_convert_fusion.3
  419.1 0.9 copy.7
  420.0 88.5 %all-gather.8.cloned.1.call-done = bf16[768,2048]{0,1:T(8,128)(2,1)} async-done(((bf16[768,256]{0,1:T(8,128)(2,1)}), bf16[768,2048]{0,1:T(8,128)(2,1)}) %all-gather.8.cloned.1.call-update) | async-done | bytes 3145744 | tf_op jit(solution)/shard_map/all_gather | solution.py:47
  508.5 4.3 fusion
  513.5 0.6 fusion.1
  514.1 1.6 fusion.12
  515.7 31.5 %reduce-scatter.3.cloned.1.call-done = bf16[256,96]{0,1:T(8,128)(2,1)} async-done(((bf16[256,768]{0,1:T(8,128)(2,1)}), bf16[256,96]{0,1:T(8,128)(2,1)}) %reduce-scatter.3.cloned.1.call-update) | async-done | bytes 49168 | tf_op jit(solution)/shard_map/reduce_scatter | solution.py:38
  (10 shorter events, 0.1 us)
Async XLA Ops:
  7.2 102.0 %all-gather.4.cloned.1.call-start = ((), (), s32[]{:S(2)}) async-start(), calls=%async_computation.2 | async-start | bytes 3538944 | tf_op jit(solution)/shard_map/all_gather | solution.py:25
  7.9 199.8 %all-gather.6.cloned.1.call-start = ((), (), s32[]{:S(2)}) async-start(), calls=%async_computation.3 | async-start | bytes 3538944 | tf_op jit(solution)/shard_map/all_gather | solution.py:22
  8.6 286.5 %all-reduce.3.cloned.1.call-start = ((), (), s32[]{:S(2)}) async-start(), calls=%async_computation.7 | async-start | bytes 4194304 | tf_op jit(solution)/shard_map/psum | solution.py:31
  211.6 202.8 %reduce-scatter.5.cloned.1.call-start = ((), (), s32[]{:S(2)}) async-start(), calls=%async_computation.5 | async-start | bytes 3538944 | tf_op jit(solution)/shard_map/reduce_scatter | solution.py:44
  300.7 113.8 %copy-start.2 = (bf16[768,2048]{1,0:T(8,128)(2,1)S(1)}, bf16[768,2048]{1,0:T(8,128)(2,1)}, u32[]{:S(2)}) copy-start(bf16[768,2048]{1,0:T(8,128)(2,1)} %all-gather.6.cloned.1.call-done) | copy-start | bytes 9437188
  300.7 207.8 %all-gather.8.cloned.1.call-start = ((), (), s32[]{:S(2)}) async-start(), calls=%async_computation.6 | async-start | bytes 3538944 | tf_op jit(solution)/shard_map/all_gather | solution.py:47
  414.4 132.8 %reduce-scatter.3.cloned.1.call-start = ((), (), s32[]{:S(2)}) async-start(), calls=%async_computation.4 | async-start | bytes 442368 | tf_op jit(solution)/shard_map/reduce_scatter | solution.py:38
  414.5 4.6 copy-start.1
  508.5 5.0 copy-start
Sparse Core Ops, SparseCore 0:
  11.2 97.9 all-gather.3
  112.2 95.4 all-gather.5
  211.7 83.3 all-reduce.2
  300.9 113.4 reduce-scatter.4
  417.9 90.5 all-gather.7
  512.0 35.1 reduce-scatter.2
where the time goes:
time: 558 us; the launch traced here: 554 us
  waiting for transfers between devices  466 us (84%)
  blocking collectives  47.6 us (9%)
  matrix products  19.6 us (4%)
  between operations  14.9 us (3%)
    reduce_scatter x1, waiting for transfers between devices, body(): lax.psum_scatter(dw_part.astype(jnp.bfloat16), 'gx', scatter_dimension=1,...  114 us
    all_gather x1, waiting for transfers between devices, body(): w_in_group = lax.all_gather(w_in, 'gx', axis=1, tiled=True)  94.5 us
    all_gather x1, waiting for transfers between devices, body(): grad_block = lax.all_gather(weight_grad, 'gx', axis=1, tiled=True)  88.5 us
    psum x1, waiting for transfers between devices, body(): lax.psum(pre_part.astype(jnp.bfloat16), 'gy').astype(jnp.float32)  83.5 us
    all_gather x1, waiting for transfers between devices, body(): lax.all_gather(w_out, 'gx', axis=0, tiled=True)  52.9 us
    reduce_scatter x1, waiting for transfers between devices, body(): lax.psum_scatter(dx_part.astype(jnp.bfloat16), 'gz', scatter_dimension=1,...  31.5 us
    all_gather x1, blocking collectives, body(): lax.all_gather(inputs, 'gz', axis=1, tiled=True)  26.4 us
    all_gather x1, blocking collectives, body(): lax.all_gather(out_grad, 'gz', axis=1, tiled=True)  21.2 us
  transfers between devices with their start and end apart: 6, of which 6 were waited for; matrix products, arithmetic and copies ran while one was open for 3% of the time, Pallas kernels for 0%

commit v1 on v0

v1 whole, which is shorter than its diff:
```python
import jax
import jax.numpy as jnp
from jax import lax
from jax.experimental import pallas as pl
from jax.experimental.pallas import tpu as pltpu
from jax.sharding import PartitionSpec as P

GELU_COEF = 0.7978845608
BF = jnp.bfloat16
F32 = jnp.float32
MESH = pl.DeviceIdType.MESH
UP = float(2.0**30)
DOWN = float(2.0**-30)


def gelu_slope(preact):
    inner = GELU_COEF * (preact + 0.044715 * preact * preact * preact)
    tanh_part = jnp.tanh(inner)
    return 0.5 * (1.0 + tanh_part) + 0.5 * preact * (1.0 - tanh_part * tanh_part) * GELU_COEF * (
        1.0 + 3.0 * 0.044715 * preact * preact
    )


def dot(a, b, ca, cb):
    return lax.dot_general(a, b, (((ca,), (cb,)), ((), ())), preferred_element_type=F32)


def kernel(
    xg_in, win, wout, dx_out, dw_out, gram_out,
    xg, wi_g, wo_g, psend, pown, crecv, ysend, yrecv, ht,
    dxacc, dxs, dxr, dxh, dxhr, dwf1, dwf3, dws, dwr, dwfin,
    gbuf, gsend, grecv, ghs, ghr, sqs, sqr,
    s_h, s_z, r_z, s_w, r_w, s_c, r_c, s_y, r_y, s_ah, r_ah, s_ac, r_ac,
    s_dw, r_dw, s_dx, r_dx, s_dxh, s_g, r_g, s_gh, s_sq, r_sq,
):
    gx = lax.axis_index("gx")
    gy = lax.axis_index("gy")
    z = lax.axis_index("gz")
    hi, xx = gx // 4, gx % 4
    yy, cc = gy // 2, gy % 2
    xp, xm = hi * 4 + (xx + 1) % 4, hi * 4 + (xx + 3) % 4
    other_hi = (1 - hi) * 4 + xx
    other_core = yy * 2 + 1 - cc
    zp, zm = (z + 1) % 8, (z + 7) % 8

    barrier = pltpu.get_barrier_semaphore()
    for k in range(1, 8):
        pl.semaphore_signal(barrier, inc=1, device_id={"gx": (gx + k) % 8}, device_id_type=MESH)
        pl.semaphore_signal(barrier, inc=1, device_id={"gz": (z + k) % 8}, device_id_type=MESH)
    for k in range(1, 4):
        pl.semaphore_signal(
            barrier, inc=1, device_id={"gy": ((yy + k) % 4) * 2 + cc}, device_id_type=MESH
        )
    pl.semaphore_signal(barrier, inc=1, device_id={"gy": other_core}, device_id_type=MESH)
    pl.semaphore_wait(barrier, 18)

    started = []

    def rc(src, dst, ssem, rsem, dev):
        return pltpu.make_async_remote_copy(
            src_ref=src, dst_ref=dst, send_sem=ssem, recv_sem=rsem,
            device_id=dev, device_id_type=MESH,
        )

    def send(src, dst, ssem, rsem, dev):
        copy = rc(src, dst, ssem, rsem, dev)
        copy.start()
        started.append(copy)

    def zrows(i):
        return pl.ds(pl.multiple_of(i * 96, 32), 96)

    own = zrows(z)
    h_dev = {"gx": other_hi}
    send(xg_in, xg.at[:, 1, own, :], s_h.at[0], s_h.at[1], h_dev)
    hops = ((4, 3), (3, 4))

    def zcopy(r, a, d, s, at=None):
        dev = zp if d == 0 else zm
        begun = (z + 8 - (s - 1)) % 8 if d == 0 else (z + s - 1) % 8
        rows = zrows(begun)
        src = xg.at[a, r, rows, :]
        if s == 1 and r == 0:
            src = xg_in.at[a]
        return src, xg.at[a, r, rows, :], s_z.at[r, a, d, s - 1], r_z.at[r, a, d, s - 1], {"gz": dev}

    def zwait(r, a, d, s):
        begun = (z + 8 - s) % 8 if d == 0 else (z + s) % 8
        rows = zrows(begun)
        ref = xg.at[a, r, rows, :]
        rc(ref, ref, s_z.at[r, a, d, s - 1], r_z.at[r, a, d, s - 1], {"gz": zp}).wait_recv()

    for a in range(2):
        for d in range(2):
            send(*zcopy(0, a, d, 1))
    send(win, wi_g.at[2], s_w.at[0], r_w.at[0], {"gx": xp})
    send(wout, wo_g.at[2], s_w.at[1], r_w.at[1], {"gx": xp})
    send(win, wi_g.at[0], s_w.at[2], r_w.at[2], {"gx": xm})
    send(wout, wo_g.at[0], s_w.at[3], r_w.at[3], {"gx": xm})
    xg[:, 0, own, :] = xg_in[...]

    rc(xg_in, xg.at[:, 1, own, :], s_h.at[0], s_h.at[1], h_dev).wait_recv()
    for a in range(2):
        for d in range(2):
            send(*zcopy(1, a, d, 1))
    for s in range(1, 5):
        for r in range(2):
            for a in range(2):
                for d in range(2):
                    if s <= hops[a][d]:
                        zwait(r, a, d, s)
                        if s < hops[a][d]:
                            send(*zcopy(r, a, d, s + 1))

    def wait_w(i):
        ref = (wi_g, wo_g)[i % 2].at[2 if i < 2 else 0]
        rc(ref, ref, s_w.at[i], r_w.at[i], {"gx": xp}).wait_recv()

    wait_w(2)
    wait_w(3)
    def w_of(c):
        return (win, wout) if c == 3 else (wi_g.at[c], wo_g.at[c])

    def half(i):
        return pl.ds(pl.multiple_of(i * 128, 128), 128)

    c_dev = {"gy": other_core}

    def part(c, side):
        wi, wo = w_of(c)
        wi_h = wi[:, half(side)]
        wo_h = wo[half(side), :]
        return [
            [dot(wi_h, xg[0, r], 0, 0) for r in range(2)],
            [dot(wo_h, xg[1, r], 1, 0) for r in range(2)],
        ]

    def stage_a(c):
        vals = part(c, 1 - cc)
        for k in range(2):
            for r in range(2):
                psend[c, k, r] = vals[k][r].astype(BF)
        send(psend.at[c], crecv.at[c], s_c.at[c], r_c.at[c], c_dev)
        vals = part(c, cc)
        for k in range(2):
            for r in range(2):
                pown[c, k, r] = vals[k][r]

    def yrows(i):
        return pl.ds(pl.multiple_of(i * 32, 32), 32)

    def stage_b(c):
        rc(psend.at[c], crecv.at[c], s_c.at[c], r_c.at[c], c_dev).wait_recv()
        total = pown[c] + crecv[c].astype(F32)
        pown[c] = total
        ysend[c] = total.astype(BF)
        for k in (1, 3, 2):
            to = (yy + k) % 4
            send(
                ysend.at[c, :, :, yrows(to), :], yrecv.at[c, k - 1],
                s_y.at[c, k - 1], r_y.at[c, k - 1], {"gy": to * 2 + cc},
            )

    def hrows(y):
        return pl.ds(pl.multiple_of(cc * 128 + y * 32, 32), 32)

    def stage_c(c):
        total = pown[c, :, :, yrows(yy), :]
        for k in range(1, 4):
            ref = yrecv.at[c, k - 1]
            rc(ref, ref, s_y.at[c, k - 1], r_y.at[c, k - 1], c_dev).wait_recv()
            total = total + yrecv[c, k - 1].astype(F32)
        ht[c, :, hrows(yy), :] = (total[1] * gelu_slope(total[0])).astype(BF)
        for k in (1, 3, 2):
            to = (yy + k) % 4
            ref = ht.at[c, :, hrows(yy), :]
            send(ref, ref, s_ah.at[c, k - 1], r_ah.at[c, k - 1], {"gy": to * 2 + cc})

    def stage_d(c):
        for k in range(1, 4):
            ref = ht.at[c, :, hrows((yy + 4 - k) % 4), :]
            rc(ref, ref, s_ah.at[c, k - 1], r_ah.at[c, k - 1], c_dev).wait_recv()
        ref = ht.at[c, :, half(cc), :]
        send(ref, ref, s_ac.at[c], r_ac.at[c], c_dev)

    def wait_dw(i, ref):
        rc(ref, ref, s_dw.at[i], r_dw.at[i], {"gx": xp}).wait_recv()

    def stage_e(c):
        ref = ht.at[c, :, half(1 - cc), :]
        rc(ref, ref, s_ac.at[c], r_ac.at[c], c_dev).wait_recv()
        wi = w_of(c)[0]
        for r in range(2):
            val = dot(wi[...], ht[c, r], 1, 0)
            dxacc[r] = val if c == 0 else dxacc[r] + val
        if c == 3:
            dxs[...] = dxacc[...].astype(BF)
            for k in (4, 3, 5, 2, 6, 1, 7):
                to = (z + k) % 8
                send(
                    dxs.at[:, zrows(to), :], dxr.at[k - 1],
                    s_dx.at[k - 1], r_dx.at[k - 1], {"gz": to},
                )
        dw = dot(xg[0, 0], ht[c, 0], 1, 1) + dot(xg[0, 1], ht[c, 1], 1, 1)
        if c == 0:
            dwf1[...] = dw[:384]
            dws[2] = dw[384:].astype(BF)
            send(dws.at[2], dwr.at[2], s_dw.at[2], r_dw.at[2], {"gx": xp})
        elif c == 1:
            dws[0] = dw[:384].astype(BF)
            dws[1] = dw[384:].astype(BF)
            send(dws.at[0], dwr.at[0], s_dw.at[0], r_dw.at[0], {"gx": xp})
            send(dws.at[1], dwr.at[1], s_dw.at[1], r_dw.at[1], {"gx": xm})
        elif c == 2:
            dws[3] = dw[:384].astype(BF)
            send(dws.at[3], dwr.at[3], s_dw.at[3], r_dw.at[3], {"gx": xm})
            dwf3[...] = dw[384:]
            wait_dw(0, dwr.at[0])
            dws[4] = (dwf1[...] + dwr[0].astype(F32)).astype(BF)
            send(dws.at[4], dwr.at[4], s_dw.at[4], r_dw.at[4], {"gx": xp})
            wait_dw(1, dwr.at[1])
            dws[5] = (dwf3[...] + dwr[1].astype(F32)).astype(BF)
            send(dws.at[5], dwr.at[5], s_dw.at[5], r_dw.at[5], {"gx": xm})
        else:
            for i in (2, 3, 4, 5):
                wait_dw(i, dwr.at[i])
            low = dw[:384] + dwr[3].astype(F32) + dwr[4].astype(F32)
            high = dw[384:] + dwr[2].astype(F32) + dwr[5].astype(F32)
            dwfin[:384, :] = low.astype(BF)
            dwfin[384:, :] = high.astype(BF)

    stage_a(0)
    wait_w(0)
    wait_w(1)
    send(wi_g.at[2], wi_g.at[1], s_w.at[4], r_w.at[4], {"gx": xp})
    send(wo_g.at[0], wo_g.at[1], s_w.at[5], r_w.at[5], {"gx": xm})
    stage_b(0)

    def wait_opposite():
        rc(wi_g.at[2], wi_g.at[1], s_w.at[4], r_w.at[4], {"gx": xp}).wait_recv()
        rc(wo_g.at[0], wo_g.at[1], s_w.at[5], r_w.at[5], {"gx": xm}).wait_recv()

    wait_opposite()
    stage_a(1)
    stage_b(1)
    stage_a(2)
    stage_b(2)
    stage_c(0)
    stage_a(3)
    stage_b(3)
    stage_d(0)
    stage_c(1)
    stage_e(0)
    stage_d(1)
    stage_c(2)
    stage_e(1)
    stage_d(2)
    stage_c(3)
    stage_e(2)
    stage_d(3)
    stage_e(3)

    w = dwfin[...]
    dw_out[...] = w
    wf = w.astype(F32)
    sqs[...] = jnp.broadcast_to(jnp.sum(wf * wf), (8, 128))
    for k in range(1, 8):
        send(sqs, sqr.at[k - 1], s_sq.at[k - 1], r_sq.at[k - 1], {"gx": (gx + k) % 8})
    ws = (wf * UP).astype(BF)
    gbuf[...] = dot(ws, ws, 1, 1).reshape(2, 4, 96, 768)
    x1, x2, x3 = (xx + 1) % 4, (xx + 2) % 4, (xx + 3) % 4

    def wait_g(i):
        rc(gsend.at[i], grecv.at[i], s_g.at[i], r_g.at[i], {"gx": xp}).wait_recv()

    def send_g(i, val, dev):
        gsend[i] = val.astype(BF)
        send(gsend.at[i], grecv.at[i], s_g.at[i], r_g.at[i], {"gx": dev})

    send_g(0, gbuf[0, x2], xp)
    send_g(1, gbuf[1, x2], xm)
    send_g(2, gbuf[1, x1], xp)
    send_g(3, gbuf[0, x3], xm)
    wait_g(0)
    send_g(4, gbuf[0, x1] + grecv[0].astype(F32), xp)
    wait_g(1)
    send_g(5, gbuf[1, x3] + grecv[1].astype(F32), xm)

    dx_tot = [dxacc[0, own, :], dxacc[1, own, :]]
    for k in (1, 7, 2, 6, 3, 5, 4):
        ref = dxr.at[k - 1]
        rc(ref, ref, s_dx.at[k - 1], r_dx.at[k - 1], c_dev).wait_recv()
        for r in range(2):
            dx_tot[r] = dx_tot[r] + dxr[k - 1, r].astype(F32)
    dxh[...] = dx_tot[1].astype(BF)
    send(dxh, dxhr, s_dxh.at[0], s_dxh.at[1], h_dev)

    for i in (2, 3, 4, 5):
        wait_g(i)
    gbuf[0, xx] = gbuf[0, xx] + grecv[3].astype(F32) + grecv[4].astype(F32)
    gbuf[1, xx] = gbuf[1, xx] + grecv[2].astype(F32) + grecv[5].astype(F32)
    ghs[...] = gbuf[1 - hi, xx].astype(BF)
    send(ghs, ghr, s_gh.at[0], s_gh.at[1], h_dev)

    rc(dxh, dxhr, s_dxh.at[0], s_dxh.at[1], h_dev).wait_recv()
    dx_out[...] = (dx_tot[0] + dxhr[...].astype(F32)).astype(BF)

    sq = sqs[...]
    for k in range(1, 8):
        rc(sqs, sqr.at[k - 1], s_sq.at[k - 1], r_sq.at[k - 1], h_dev).wait_recv()
        sq = sq + sqr[k - 1]
    factor = DOWN / (jnp.sqrt(sq[:1, :1]) + 1e-07)
    rc(ghs, ghr, s_gh.at[0], s_gh.at[1], h_dev).wait_recv()
    gram_out[...] = (gbuf[hi, xx] + ghr[...].astype(F32)) * factor * factor * 768.0

    for copy in started:
        copy.wait_send()


def body(inputs, out_grad, w_in, w_out):
    xg_in = jnp.stack([inputs.T, out_grad.T])
    vmem = pl.BlockSpec(memory_space=pltpu.VMEM)
    dma = pltpu.SemaphoreType.DMA
    dx_t, weight_grad, gram = pl.pallas_call(
        kernel,
        out_shape=(
            jax.ShapeDtypeStruct((96, 256), BF),
            jax.ShapeDtypeStruct((768, 256), BF),
            jax.ShapeDtypeStruct((96, 768), F32),
        ),
        in_specs=[vmem] * 3,
        out_specs=(vmem,) * 3,
        scratch_shapes=[
            pltpu.VMEM((2, 2, 768, 256), BF),
            pltpu.VMEM((3, 768, 256), BF),
            pltpu.VMEM((3, 256, 768), BF),
            pltpu.VMEM((4, 2, 2, 128, 256), BF),
            pltpu.VMEM((4, 2, 2, 128, 256), F32),
            pltpu.VMEM((4, 2, 2, 128, 256), BF),
            pltpu.VMEM((4, 2, 2, 128, 256), BF),
            pltpu.VMEM((4, 3, 2, 2, 32, 256), BF),
            pltpu.VMEM((4, 2, 256, 256), BF),
            pltpu.VMEM((2, 768, 256), F32),
            pltpu.VMEM((2, 768, 256), BF),
            pltpu.VMEM((7, 2, 96, 256), BF),
            pltpu.VMEM((96, 256), BF),
            pltpu.VMEM((96, 256), BF),
            pltpu.VMEM((384, 256), F32),
            pltpu.VMEM((384, 256), F32),
            pltpu.VMEM((6, 384, 256), BF),
            pltpu.VMEM((6, 384, 256), BF),
            pltpu.VMEM((768, 256), BF),
            pltpu.VMEM((2, 4, 96, 768), F32),
            pltpu.VMEM((6, 96, 768), BF),
            pltpu.VMEM((6, 96, 768), BF),
            pltpu.VMEM((96, 768), BF),
            pltpu.VMEM((96, 768), BF),
            pltpu.VMEM((8, 128), F32),
            pltpu.VMEM((7, 8, 128), F32),
            dma((2,)), dma((2, 2, 2, 4)), dma((2, 2, 2, 4)), dma((6,)), dma((6,)),
            dma((4,)), dma((4,)), dma((4, 3)), dma((4, 3)), dma((4, 3)), dma((4, 3)),
            dma((4,)), dma((4,)), dma((6,)), dma((6,)), dma((7,)), dma((7,)), dma((2,)),
            dma((6,)), dma((6,)), dma((2,)), dma((7,)), dma((7,)),
        ],
        compiler_params=pltpu.CompilerParams(
            collective_id=0, has_side_effects=True, vmem_limit_bytes=48 * 1024 * 1024
        ),
        cost_estimate=pl.CostEstimate(
            flops=3_600_000_000, bytes_accessed=4_000_000, transcendentals=131072
        ),
    )(xg_in, w_in, w_out)
    return (dx_t.T, weight_grad, gram[None])


def solution(mesh):
    placed = (
        P("gx", ("gy", "gz")),
        P("gx", ("gy", "gz")),
        P("gy", ("gx", "gz")),
        P(("gx", "gz"), "gy"),
    )
    return jax.shard_map(
        body,
        mesh=mesh,
        in_specs=placed,
        out_specs=(P("gx", ("gy", "gz")), P("gy", ("gx", "gz")), P("gz", ("gy", "gx"), None)),
        check_vma=False,
    )
```

time: 558 us -> 124 us (0.22)
  waiting for transfers between devices: 466 us -> 0 us
  Pallas kernels: 0 us -> 118 us
  blocking collectives: 47.6 us -> 0 us
  matrix products: 19.6 us -> 0 us
  between operations: 14.9 us -> 0.65 us
    all_gather x3 -> x0, waiting for transfers between devices: 236 us -> none  [the longest x1 94.5 us: body(): w_in_group = lax.all_gather(w_in, 'gx', axis=1, tiled=True)]
    reduce_scatter x2 -> x0, waiting for transfers between devices: 145 us -> none  [the longest x1 114 us: body(): lax.psum_scatter(dw_part.astype(jnp.bfloat16), 'gx', scatter_dimension=1,...]
    pallas_call x0 -> x1, Pallas kernels: none -> 118 us  [body(): pl.pallas_call(kernel, out_shape=(jax.ShapeDtypeStruct((96, 256), BF), ja...]
    psum x1 -> x0, waiting for transfers between devices: 83.5 us -> none  [body(): lax.psum(pre_part.astype(jnp.bfloat16), 'gy').astype(jnp.float32)]
    all_gather x2 -> x0, blocking collectives: 47.6 us -> none  [the longest x1 26.4 us: body(): lax.all_gather(inputs, 'gz', axis=1, tiled=True)]
    dot_general x5 -> x0, matrix products: 19.6 us -> none  [the longest x1 5.55 us: body(): lax.dot_general(x_rows, hidden_grad, (((0,), (0,)), ((), ())), preferred_...]
  transfers between devices with their start and end apart: 6 -> 0, of which waited for: 6 -> 0; matrix products, arithmetic and copies ran while one was open for 3% -> 0% of each run, Pallas kernels for 0% -> 0%
where the time goes in v1:
time: 124 us
  Pallas kernels  118 us (95%)
  local copies, waits for them, and re-layouts  4.07 us (3%)
    pallas_call x1, Pallas kernels, body(): pl.pallas_call(kernel, out_shape=(jax.ShapeDtypeStruct((96, 256), BF), ja...  118 us
    unnamed x7, local copies, waits for them, and re-layouts  4.07 us

profile of v1, /device:TPU:1, one launch (start us, length us, event | category | flops | bytes accessed | tf_op | source)
XLA Modules:
  0.0 123.6 jit_solution(1294669327485702774)
XLA Ops:
  0.6 0.8 pad_maximum_fusion.xg_in
  1.5 0.0 copy-start
  1.5 1.0 copy-done
  2.5 0.0 copy-start.1
  2.5 1.0 copy-done.1
  3.5 118.1 %shard_map.67 = (bf16[96,256]{1,0:T(8,128)(2,1)S(1)}, bf16[768,256]{1,0:T(8,128)(2,1)S(1)}, f32[96,768]{1,0:T(8,128)S(1)}) custom-call(bf16[2,96,256]{2,1,0:T(8,128)(2,1)S(1)} %pad_maximum_fusion.xg_in, bf16[768,256]{1,0:T(8,128)(2,1)S(1)} %copy-done, bf16[256,768]{1,0:T(8,128)(2,1)S(1)} %copy-done.1), custom_call_target="tpu_custom_call" | custom-call | flops 3600000000 | bytes 4000000 | tf_op jit(solution)/shard_map/pallas_call | solution.py:324
  121.5 0.6 copy.10
  122.2 0.7 copy.11
  122.9 0.7 copy.12
Async XLA Ops:
  1.5 1.0 copy-start
  2.5 1.0 copy-start.1

commit v2 on v0

v2 whole, which is shorter than its diff:
```python
import jax
import jax.numpy as jnp
from jax import lax
from jax.experimental import pallas as pl
from jax.experimental.pallas import tpu as pltpu
from jax.sharding import PartitionSpec as P

GELU_COEF = 0.7978845608
BF = jnp.bfloat16
F32 = jnp.float32
MESH = pl.DeviceIdType.MESH
UP = float(2.0**30)
DOWN = float(2.0**-30)
NH = 2
CH = 256 // NH
NP = 3
SLOTS = 288

ORDER = [
    (0, 0, 0), (0, 1, 0), (1, 0, 0), (3, 0, 0), (1, 0, 1), (3, 0, 1), (1, 1, 0), (3, 1, 0),
    (1, 1, 1), (3, 1, 1), (2, 0, 0), (2, 0, 1), (2, 1, 0), (2, 1, 1), (0, 0, 1), (0, 1, 1),
]
LAG_B, LAG_B2, LAG_C, LAG_D, LAG_E = 1, 3, 5, 7, 8


def gelu_slope(preact):
    inner = GELU_COEF * (preact + 0.044715 * preact * preact * preact)
    tanh_part = jnp.tanh(inner)
    return 0.5 * (1.0 + tanh_part) + 0.5 * preact * (1.0 - tanh_part * tanh_part) * GELU_COEF * (
        1.0 + 3.0 * 0.044715 * preact * preact
    )


def dot(a, b, ca, cb):
    return lax.dot_general(a, b, (((ca,), (cb,)), ((), ())), preferred_element_type=F32)


def kernel(
    x_in, g_in, win, wout, dx_out, dw_out, gram_out,
    xin, xg, wi, wo, psend, pown, crecv, ysend, yrecv, y2send, y2recv, ht,
    dxacc, dxs, dxr, dxh, dxhr, dwf, dwf0, dws, dwr,
    gbuf, gsend, grecv, ghs, ghr, sqs, sqr, l_sem, s_all, r_all,
):
    gx = lax.axis_index("gx")
    gy = lax.axis_index("gy")
    z = lax.axis_index("gz")
    hi, xx = gx // 4, gx % 4
    yy, cc = gy // 2, gy % 2
    b0, b1 = yy % 2, yy // 2
    xp = {"gx": hi * 4 + (xx + 1) % 4}
    xm = {"gx": hi * 4 + (xx + 3) % 4}
    h_dev = {"gx": (1 - hi) * 4 + xx}
    c_dev = {"gy": yy * 2 + 1 - cc}
    y1_dev = {"gy": (b1 * 2 + 1 - b0) * 2 + cc}
    y2_dev = {"gy": ((1 - b1) * 2 + b0) * 2 + cc}
    y3_dev = {"gy": ((1 - b1) * 2 + 1 - b0) * 2 + cc}
    zp, zm = {"gz": (z + 1) % 8}, {"gz": (z + 7) % 8}

    barrier = pltpu.get_barrier_semaphore()
    partners = [{"gx": (gx + k) % 8} for k in range(1, 8)]
    partners += [{"gz": (z + k) % 8} for k in range(1, 8)]
    partners += [c_dev, y1_dev, y2_dev, y3_dev]
    for dev in partners:
        pl.semaphore_signal(barrier, inc=1, device_id=dev, device_id_type=MESH)

    slots = {}
    started = []

    def rc(src, dst, name, dev):
        slot = slots.setdefault(name, len(slots))
        return pltpu.make_async_remote_copy(
            src_ref=src, dst_ref=dst, send_sem=s_all.at[slot], recv_sem=r_all.at[slot],
            device_id=dev, device_id_type=MESH,
        )

    def send(src, dst, name, dev):
        copy = rc(src, dst, name, dev)
        copy.start()
        started.append(copy)

    def arrived(ref, name):
        rc(ref, ref, name, c_dev).wait_recv()

    def zrows(i):
        return pl.ds(pl.multiple_of(i * 96, 32), 96)

    own = zrows(z)
    local = [
        pltpu.make_async_copy(x_in, xin.at[0], l_sem.at[0]),
        pltpu.make_async_copy(g_in, xin.at[1], l_sem.at[1]),
        pltpu.make_async_copy(win, wi.at[0], l_sem.at[2]),
        pltpu.make_async_copy(wout, wo.at[0], l_sem.at[3]),
    ]
    for copy in local:
        copy.start()
    for a in range(2):
        local[a].wait()
        xg[a, 0, own, :] = xin[a].T
    pl.semaphore_wait(barrier, len(partners))

    hops = ((4, 3), (3, 4))

    def zref(r, a, d, s):
        begun = (z + 8 - s) % 8 if d == 0 else (z + s) % 8
        return xg.at[a, r, zrows(begun), :]

    def zsend(r, a, d, s):
        ref = zref(r, a, d, s - 1)
        send(ref, ref, ("z", r, a, d, s), zp if d == 0 else zm)

    def zstep(r, s):
        for a in range(2):
            for d in range(2):
                if s <= hops[a][d]:
                    arrived(zref(r, a, d, s), ("z", r, a, d, s))
                    if s < hops[a][d]:
                        zsend(r, a, d, s + 1)

    def hstep():
        for a in range(2):
            arrived(xg.at[a, 1, own, :], ("h", a))
            for d in range(2):
                zsend(1, a, d, 1)

    for a in range(2):
        send(xg.at[a, 0, own, :], xg.at[a, 1, own, :], ("h", a), h_dev)
        for d in range(2):
            zsend(0, a, d, 1)

    def piece(b):
        return pl.ds(b * CH, CH)

    for b in range(NH):
        send(win.at[:, piece(b)], wi.at[3, :, piece(b)], ("w", b, 0), xp)
        send(win.at[:, piece(b)], wi.at[1, :, piece(b)], ("w", b, 2), xm)
        send(wout.at[piece(b), :], wo.at[3, piece(b), :], ("w", b, 1), xp)
        send(wout.at[piece(b), :], wo.at[1, piece(b), :], ("w", b, 3), xm)

    def w_near(b):
        arrived(wi.at[3, :, piece(b)], ("w", b, 0))
        send(wi.at[3, :, piece(b)], wi.at[2, :, piece(b)], ("w", b, 4), xp)
        arrived(wo.at[1, piece(b), :], ("w", b, 3))
        send(wo.at[1, piece(b), :], wo.at[2, piece(b), :], ("w", b, 5), xm)
        arrived(wi.at[1, :, piece(b)], ("w", b, 2))
        arrived(wo.at[3, piece(b), :], ("w", b, 1))

    def w_far(b):
        arrived(wi.at[2, :, piece(b)], ("w", b, 4))
        arrived(wo.at[2, piece(b), :], ("w", b, 5))

    zstep(0, 1)
    hstep()
    zstep(0, 2)
    zstep(1, 1)
    zstep(0, 3)
    zstep(0, 4)
    local[2].wait()
    local[3].wait()

    def rows(i, n):
        return pl.ds(pl.multiple_of(i * n, n), n)

    def stage_a(c):
        s, b, r = ORDER[c]
        pre = dot(wi[s, :, b * CH : (b + 1) * CH], xg[0, r], 0, 0)
        back = dot(wo[s, b * CH : (b + 1) * CH, :], xg[1, r], 1, 0)
        for k, val in enumerate((pre, back)):
            pown[c, k] = val
            psend[c, k] = val.astype(BF)
        send(psend.at[c, :, rows(1 - cc, CH // 2), :], crecv.at[c], ("c", c), c_dev)

    def stage_b(c):
        arrived(crecv.at[c], ("c", c))
        total = pown[c, :, rows(cc, CH // 2), :] + crecv[c].astype(F32)
        pown[c, :, : CH // 2, :] = total
        ysend[c] = total.astype(BF)
        send(ysend.at[c, :, rows(1 - b0, CH // 4), :], yrecv.at[c], ("y", c), y1_dev)

    def stage_b2(c):
        arrived(yrecv.at[c], ("y", c))
        total = pown[c, :, rows(b0, CH // 4), :] + yrecv[c].astype(F32)
        pown[c, :, : CH // 4, :] = total
        y2send[c] = total.astype(BF)
        send(y2send.at[c, :, rows(1 - b1, CH // 8), :], y2recv.at[c], ("y2", c), y2_dev)

    def hrows(p0, p1):
        return rows(cc * 4 + p0 * 2 + p1, CH // 8)

    def stage_c(c):
        arrived(y2recv.at[c], ("y2", c))
        total = pown[c, :, rows(b1, CH // 8), :] + y2recv[c].astype(F32)
        ht[c, hrows(b0, b1), :] = (total[1] * gelu_slope(total[0])).astype(BF)
        ref = ht.at[c, hrows(b0, b1), :]
        for k, dev in ((1, y1_dev), (2, y2_dev), (3, y3_dev)):
            send(ref, ref, ("ah", c, k), dev)

    def stage_d(c):
        arrived(ht.at[c, hrows(1 - b0, b1), :], ("ah", c, 1))
        arrived(ht.at[c, hrows(b0, 1 - b1), :], ("ah", c, 2))
        arrived(ht.at[c, hrows(1 - b0, 1 - b1), :], ("ah", c, 3))
        ref = ht.at[c, rows(cc, CH // 2), :]
        send(ref, ref, ("ac", c), c_dev)

    done = set()
    seen = [0, 0]

    def stage_e(c):
        s, b, r = ORDER[c]
        arrived(ht.at[c, rows(1 - cc, CH // 2), :], ("ac", c))
        val = dot(wi[s, :, b * CH : (b + 1) * CH], ht[c], 1, 0)
        dxacc[r] = val if seen[r] == 0 else dxacc[r] + val
        seen[r] += 1
        if seen[r] == 4 * NH:
            dxs[r] = dxacc[r].astype(BF)
            for k in (4, 3, 5, 2, 6, 1, 7):
                to = (z + k) % 8
                send(dxs.at[r, zrows(to), :], dxr.at[r, k - 1], ("dx", r, k), {"gz": to})
        done.add((s, b, r))
        if (s, b, 1 - r) not in done:
            return
        c0, c1 = ORDER.index((s, b, 0)), ORDER.index((s, b, 1))
        dw = dot(xg[0, 0], ht[c0], 1, 1) + dot(xg[0, 1], ht[c1], 1, 1)
        if s == 0:
            dwf0[b] = dw
        elif s == 1:
            dwf[b, 0] = dw[:384]
            put_dw(b, 2, dw[384:], xp)
        elif s == 2:
            put_dw(b, 0, dw[:384], xp)
            put_dw(b, 1, dw[384:], xm)
        else:
            dwf[b, 1] = dw[384:]
            put_dw(b, 3, dw[:384], xm)

    def put_dw(b, i, val, dev):
        dws[b, i] = val.astype(BF)
        send(dws.at[b, i], dwr.at[b, i], ("dw", b, i), dev)

    def add_dw(b):
        for i, dev in ((0, xp), (1, xm)):
            arrived(dwr.at[b, i], ("dw", b, i))
            put_dw(b, 4 + i, dwf[b, i] + dwr[b, i].astype(F32), dev)

    def own_dw(b):
        for i in (2, 3, 4, 5):
            arrived(dwr.at[b, i], ("dw", b, i))
        low = dwf0[b, :384] + dwr[b, 3].astype(F32) + dwr[b, 4].astype(F32)
        high = dwf0[b, 384:] + dwr[b, 2].astype(F32) + dwr[b, 5].astype(F32)
        dw_out[:384, b * CH : (b + 1) * CH] = low.astype(BF)
        dw_out[384:, b * CH : (b + 1) * CH] = high.astype(BF)

    before = {1: [lambda: zstep(1, 2)], 2: [lambda: w_near(0), lambda: zstep(1, 3)],
              4: [lambda: zstep(1, 4)], 6: [lambda: w_near(1)], 10: [lambda: w_far(0)], 12: [lambda: w_far(1)]}
    after = {13: [lambda: add_dw(0)], 14: [lambda: add_dw(1)]}
    n = len(ORDER)
    for tick in range(n + LAG_E):
        for lag, stage in ((0, stage_a), (LAG_B, stage_b), (LAG_B2, stage_b2), (LAG_C, stage_c), (LAG_D, stage_d), (LAG_E, stage_e)):
            c = tick - lag
            if 0 <= c < n:
                if lag == 0:
                    for act in before.get(c, ()):
                        act()
                stage(c)
                if lag == LAG_E:
                    for act in after.get(c, ()):
                        act()
    for b in range(NH):
        own_dw(b)

    wf = dw_out[...].astype(F32)
    sqs[...] = jnp.broadcast_to(jnp.sum(wf * wf), (8, 128))
    for k in range(1, 8):
        send(sqs, sqr.at[k - 1], ("sq", k), {"gx": (gx + k) % 8})
    ws = (wf * UP).astype(BF)
    x1, x2, x3 = (xx + 1) % 4, (xx + 2) % 4, (xx + 3) % 4
    width = 768 // NP

    def put_g(p, i, val, dev):
        gsend[p, i] = val.astype(BF)
        send(gsend.at[p, i], grecv.at[p, i], ("g", p, i), dev)

    def gram_part(p):
        gbuf[p] = dot(ws, ws[p * width : (p + 1) * width], 1, 1).reshape(2, 4, 96, width)
        put_g(p, 0, gbuf[p, 0, x2], xp)
        put_g(p, 1, gbuf[p, 1, x2], xm)
        put_g(p, 2, gbuf[p, 1, x1], xp)
        put_g(p, 3, gbuf[p, 0, x3], xm)

    def gram_add(p):
        arrived(grecv.at[p, 0], ("g", p, 0))
        put_g(p, 4, gbuf[p, 0, x1] + grecv[p, 0].astype(F32), xp)
        arrived(grecv.at[p, 1], ("g", p, 1))
        put_g(p, 5, gbuf[p, 1, x3] + grecv[p, 1].astype(F32), xm)

    def gram_own(p):
        for i in (2, 3, 4, 5):
            arrived(grecv.at[p, i], ("g", p, i))
        gbuf[p, 0, xx] = gbuf[p, 0, xx] + grecv[p, 3].astype(F32) + grecv[p, 4].astype(F32)
        gbuf[p, 1, xx] = gbuf[p, 1, xx] + grecv[p, 2].astype(F32) + grecv[p, 5].astype(F32)
        ghs[p] = gbuf[p, 1 - hi, xx].astype(BF)
        send(ghs.at[p], ghr.at[p], ("gh", p), h_dev)

    def dx_sum(r):
        total = dxacc[r, own, :]
        for k in (1, 7, 2, 6, 3, 5, 4):
            arrived(dxr.at[r, k - 1], ("dx", r, k))
            total = total + dxr[r, k - 1].astype(F32)
        return total

    gram_part(0)
    gram_part(1)
    gram_add(0)
    gram_part(2)
    gram_add(1)
    gram_add(2)
    gram_own(0)
    dxh[...] = dx_sum(1).astype(BF)
    send(dxh, dxhr, ("dxh",), h_dev)
    gram_own(1)
    gram_own(2)
    dx_own = dx_sum(0)
    arrived(dxhr, ("dxh",))
    dx_out[...] = (dx_own + dxhr[...].astype(F32)).astype(BF)

    sq = sqs[...]
    for k in range(1, 8):
        arrived(sqr.at[k - 1], ("sq", k))
        sq = sq + sqr[k - 1]
    factor = DOWN / (jnp.sqrt(sq[:1, :1]) + 1e-07)
    for p in range(NP):
        arrived(ghr.at[p], ("gh", p))
        val = (gbuf[p, hi, xx] + ghr[p].astype(F32)) * factor * factor * 768.0
        gram_out[:, p * width : (p + 1) * width] = val

    for copy in started:
        copy.wait_send()


def body(inputs, out_grad, w_in, w_out):
    vmem = pl.BlockSpec(memory_space=pltpu.VMEM)
    hbm = pl.BlockSpec(memory_space=pl.ANY)
    dma = pltpu.SemaphoreType.DMA
    n = len(ORDER)
    width = 768 // NP
    dx_t, weight_grad, gram = pl.pallas_call(
        kernel,
        out_shape=(
            jax.ShapeDtypeStruct((96, 256), BF),
            jax.ShapeDtypeStruct((768, 256), BF),
            jax.ShapeDtypeStruct((96, 768), F32),
        ),
        in_specs=[hbm] * 4,
        out_specs=(vmem,) * 3,
        scratch_shapes=[
            pltpu.VMEM((2, 256, 96), BF),
            pltpu.VMEM((2, 2, 768, 256), BF),
            pltpu.VMEM((4, 768, 256), BF),
            pltpu.VMEM((4, 256, 768), BF),
            pltpu.VMEM((n, 2, CH, 256), BF),
            pltpu.VMEM((n, 2, CH, 256), F32),
            pltpu.VMEM((n, 2, CH // 2, 256), BF),
            pltpu.VMEM((n, 2, CH // 2, 256), BF),
            pltpu.VMEM((n, 2, CH // 4, 256), BF),
            pltpu.VMEM((n, 2, CH // 4, 256), BF),
            pltpu.VMEM((n, 2, CH // 8, 256), BF),
            pltpu.VMEM((n, CH, 256), BF),
            pltpu.VMEM((2, 768, 256), F32),
            pltpu.VMEM((2, 768, 256), BF),
            pltpu.VMEM((2, 7, 96, 256), BF),
            pltpu.VMEM((96, 256), BF),
            pltpu.VMEM((96, 256), BF),
            pltpu.VMEM((NH, 2, 384, CH), F32),
            pltpu.VMEM((NH, 768, CH), F32),
            pltpu.VMEM((NH, 6, 384, CH), BF),
            pltpu.VMEM((NH, 6, 384, CH), BF),
            pltpu.VMEM((NP, 2, 4, 96, width), F32),
            pltpu.VMEM((NP, 6, 96, width), BF),
            pltpu.VMEM((NP, 6, 96, width), BF),
            pltpu.VMEM((NP, 96, width), BF),
            pltpu.VMEM((NP, 96, width), BF),
            pltpu.VMEM((8, 128), F32),
            pltpu.VMEM((7, 8, 128), F32),
            dma((4,)), dma((SLOTS,)), dma((SLOTS,)),
        ],
        compiler_params=pltpu.CompilerParams(
            collective_id=0, has_side_effects=True, vmem_limit_bytes=48 * 1024 * 1024
        ),
        cost_estimate=pl.CostEstimate(
            flops=3_600_000_000, bytes_accessed=4_000_000, transcendentals=131072
        ),
    )(inputs, out_grad, w_in, w_out)
    return (dx_t.T, weight_grad, gram[None])


def solution(mesh):
    placed = (
        P("gx", ("gy", "gz")),
        P("gx", ("gy", "gz")),
        P("gy", ("gx", "gz")),
        P(("gx", "gz"), "gy"),
    )
    return jax.shard_map(
        body,
        mesh=mesh,
        in_specs=placed,
        out_specs=(P("gx", ("gy", "gz")), P("gy", ("gx", "gz")), P("gz", ("gy", "gx"), None)),
        check_vma=False,
    )
```

time: 558 us -> 110 us (0.20)
  waiting for transfers between devices: 466 us -> 0 us
  Pallas kernels: 0 us -> 104 us
  blocking collectives: 47.6 us -> 0 us
  matrix products: 19.6 us -> 0 us
  between operations: 14.9 us -> 0.68 us
    all_gather x3 -> x0, waiting for transfers between devices: 236 us -> none  [the longest x1 94.5 us: body(): w_in_group = lax.all_gather(w_in, 'gx', axis=1, tiled=True)]
    reduce_scatter x2 -> x0, waiting for transfers between devices: 145 us -> none  [the longest x1 114 us: body(): lax.psum_scatter(dw_part.astype(jnp.bfloat16), 'gx', scatter_dimension=1,...]
    pallas_call x0 -> x1, Pallas kernels: none -> 104 us  [body(): pl.pallas_call(kernel, out_shape=(jax.ShapeDtypeStruct((96, 256), BF), ja...]
    psum x1 -> x0, waiting for transfers between devices: 83.5 us -> none  [body(): lax.psum(pre_part.astype(jnp.bfloat16), 'gy').astype(jnp.float32)]
    all_gather x2 -> x0, blocking collectives: 47.6 us -> none  [the longest x1 26.4 us: body(): lax.all_gather(inputs, 'gz', axis=1, tiled=True)]
    dot_general x5 -> x0, matrix products: 19.6 us -> none  [the longest x1 5.55 us: body(): lax.dot_general(x_rows, hidden_grad, (((0,), (0,)), ((), ())), preferred_...]
  transfers between devices with their start and end apart: 6 -> 0, of which waited for: 6 -> 0; matrix products, arithmetic and copies ran while one was open for 3% -> 0% of each run, Pallas kernels for 0% -> 0%
where the time goes in v2:
time: 110 us
  Pallas kernels  104 us (95%)
  local copies, waits for them, and re-layouts  5.11 us (5%)
    pallas_call x1, Pallas kernels, body(): pl.pallas_call(kernel, out_shape=(jax.ShapeDtypeStruct((96, 256), BF), ja...  104 us
    unnamed x11, local copies, waits for them, and re-layouts  5.11 us

profile of v2, /device:TPU:1, one launch (start us, length us, event | category | flops | bytes accessed | tf_op | source)
XLA Modules:
  0.0 109.8 jit_solution(13308531050824896332)
XLA Ops:
  0.6 0.0 copy-start.2
  0.6 0.9 copy.7.x_in
  1.6 0.0 copy-done.2
  1.6 0.1 copy.8.g_in
  1.7 0.0 copy-start
  1.7 1.0 copy-done
  2.7 0.0 copy-start.1
  2.7 1.0 copy-done.1
  3.7 104.0 %shard_map.67 = (bf16[96,256]{1,0:T(8,128)(2,1)S(1)}, bf16[768,256]{1,0:T(8,128)(2,1)S(1)}, f32[96,768]{1,0:T(8,128)S(1)}) custom-call(bf16[256,96]{1,0:T(8,128)(2,1)S(1)} %copy.7.x_in, bf16[256,96]{1,0:T(8,128)(2,1)S(1)} %copy.8.g_in, bf16[768,256]{1,0:T(8,128)(2,1)S(1)} %copy-done, bf16[256,768]{1,0:T(8,128)(2,1)S(1)} %copy-done.1), custom_call_target="tpu_custom_call" | custom-call | flops 3600000000 | bytes 4000000 | tf_op jit(solution)/shard_map/pallas_call | solution.py:345
  107.7 0.6 copy.12
  108.3 0.7 copy.13
  109.1 0.7 copy.14
Async XLA Ops:
  0.6 0.9 copy-start.2
  1.7 1.0 copy-start
  2.7 1.0 copy-start.1

commit v3 on v2

v3 whole, which is shorter than its diff:
```python
import jax
import jax.numpy as jnp
from jax import lax
from jax.experimental import pallas as pl
from jax.experimental.pallas import tpu as pltpu
from jax.sharding import PartitionSpec as P

GELU_COEF = 0.7978845608
BF = jnp.bfloat16
F32 = jnp.float32
MESH = pl.DeviceIdType.MESH
UP = float(2.0**30)
DOWN = float(2.0**-30)
NH = 2
CH = 256 // NH
NP = 3
KINDS = 16
SLOTS = 160
TOGETHER = {"ah": 2, "dx": 2, "sq": 1}

SCHEDULE = [
    ("start",), ("wstart", 0), ("z", 0, 1, 1, 1), ("z", 0, 0, 0, 1), ("wstart", 1), ("z", 0, 1, 0, 1), ("hs", 0),
    ("z", 0, 0, 1, 1), ("z", 0, 1, 1, 2), ("z", 0, 0, 0, 2), ("hs", 1), ("z", 0, 0, 1, 2), ("z", 1, 0, 0, 1),
    ("z", 0, 0, 0, 3), ("z", 0, 1, 0, 2), ("z", 0, 1, 1, 3), ("z", 1, 1, 1, 1), ("wf", 0, 0), ("z", 1, 0, 1, 1),
    ("z", 1, 0, 0, 2), ("z", 0, 0, 0, 4), ("z", 0, 0, 1, 3), ("wf", 0, 1), ("z", 1, 1, 1, 2), ("z", 0, 1, 0, 3),
    ("z", 0, 1, 1, 4), ("A", 3, 0, 0), ("z", 1, 1, 0, 1), ("A", 1, 0, 0), ("z", 1, 0, 1, 2), ("B", 3, 0, 0),
    ("z", 1, 0, 0, 3), ("B", 1, 0, 0), ("wf", 1, 0), ("A", 0, 1, 0), ("A", 3, 1, 0), ("wf", 1, 1), ("z", 1, 1, 1, 3),
    ("z", 1, 1, 0, 2), ("B", 3, 1, 0), ("z", 1, 0, 0, 4), ("A", 1, 1, 0), ("A", 0, 0, 0), ("z", 1, 0, 1, 3),
    ("B2", 3, 0, 0), ("B", 1, 1, 0), ("B", 0, 1, 0), ("B2", 1, 0, 0), ("z", 1, 1, 1, 4), ("A", 2, 0, 0),
    ("B2", 3, 1, 0), ("z", 1, 1, 0, 3), ("A", 1, 0, 1), ("B", 2, 0, 0), ("A", 2, 0, 1), ("B", 1, 0, 1),
    ("A", 3, 0, 1), ("B", 2, 0, 1), ("B", 3, 0, 1), ("B2", 1, 1, 0), ("A", 3, 1, 1), ("C", 3, 0, 0), ("A", 2, 1, 1),
    ("B2", 2, 0, 0), ("A", 2, 1, 0), ("C", 1, 0, 0), ("A", 1, 1, 1), ("B", 2, 1, 1), ("B2", 2, 0, 1), ("B", 2, 1, 0),
    ("B2", 3, 0, 1), ("A", 0, 0, 1), ("A", 0, 1, 1), ("B", 1, 1, 1), ("B2", 1, 0, 1), ("B", 3, 1, 1), ("C", 2, 0, 0),
    ("B2", 2, 1, 1), ("D", 3, 0, 0), ("C", 2, 0, 1), ("B2", 2, 1, 0), ("C", 3, 0, 1), ("C", 1, 0, 1), ("B", 0, 0, 1),
    ("B", 0, 1, 1), ("B2", 3, 1, 1), ("C", 3, 1, 0), ("C", 2, 1, 1), ("D", 2, 0, 0), ("D", 1, 0, 0), ("D", 2, 0, 1),
    ("C", 2, 1, 0), ("E", 1, 0, 0), ("E", 2, 0, 0), ("B2", 1, 1, 1), ("B2", 0, 0, 1), ("D", 3, 0, 1), ("E", 2, 0, 1),
    ("dw", 2, 0), ("B2", 0, 1, 1), ("D", 1, 0, 1), ("C", 1, 1, 0), ("C", 3, 1, 1), ("E", 3, 0, 0), ("B2", 0, 1, 0),
    ("E", 3, 0, 1), ("E", 1, 0, 1), ("dw", 3, 0), ("B", 0, 0, 0), ("dw", 1, 0), ("C", 1, 1, 1), ("D", 2, 1, 0),
    ("D", 2, 1, 1), ("C", 0, 0, 1), ("E", 2, 1, 0), ("E", 2, 1, 1), ("dw", 2, 1), ("C", 0, 1, 1), ("D", 3, 1, 0),
    ("add", 0, 1), ("B2", 0, 0, 0), ("E", 3, 1, 0), ("add", 0, 0), ("C", 0, 1, 0), ("D", 3, 1, 1), ("D", 1, 1, 0),
    ("D", 1, 1, 1), ("E", 3, 1, 1), ("dw", 3, 1), ("E", 1, 1, 0), ("E", 1, 1, 1), ("dw", 1, 1), ("D", 0, 0, 1),
    ("C", 0, 0, 0), ("D", 0, 1, 1), ("add", 1, 1), ("add", 1, 0), ("E", 0, 0, 1), ("E", 0, 1, 1), ("dx", 1),
    ("D", 0, 1, 0), ("E", 0, 1, 0), ("dw", 0, 1), ("D", 0, 0, 0), ("E", 0, 0, 0), ("dw", 0, 0), ("own", 0),
    ("own", 1), ("sq",), ("g", 0), ("g", 2), ("g", 1), ("g2", 0), ("dx", 0), ("ga", 0, 0), ("ga", 0, 1), ("g2", 1),
    ("dxs", 1), ("ga", 1, 1), ("ga", 2, 1), ("ga", 1, 0), ("ga", 2, 0), ("go", 0), ("g2", 2), ("go", 1), ("go", 2),
    ("dxs", 0), ("gf", 0), ("gf", 1), ("dxf",), ("gf", 2),
]


def index(s, b, r):
    return (s * NH + b) * 2 + r


def gelu_slope(preact):
    inner = GELU_COEF * (preact + 0.044715 * preact * preact * preact)
    tanh_part = jnp.tanh(inner)
    return 0.5 * (1.0 + tanh_part) + 0.5 * preact * (1.0 - tanh_part * tanh_part) * GELU_COEF * (
        1.0 + 3.0 * 0.044715 * preact * preact
    )


def dot(a, b, ca, cb):
    return lax.dot_general(a, b, (((ca,), (cb,)), ((), ())), preferred_element_type=F32)


def kernel(
    x_in, g_in, win, wout, dx_out, dw_out, gram_out,
    xg, wi, wo, psend, pown, crecv, ysend, yrecv, y2send, y2recv, ht,
    dxacc, dxo, dxs, dxr, dxh, dxhr, dwf, dwf0, dws, dwr,
    gbuf, gsend, grecv, ghs, ghr, sqs, sqr, l_sem, s_all, r_all,
):
    gx = lax.axis_index("gx")
    gy = lax.axis_index("gy")
    z = lax.axis_index("gz")
    hi, xx = gx // 4, gx % 4
    yy, cc = gy // 2, gy % 2
    b0, b1 = yy % 2, yy // 2
    xp = {"gx": hi * 4 + (xx + 1) % 4}
    xm = {"gx": hi * 4 + (xx + 3) % 4}
    h_dev = {"gx": (1 - hi) * 4 + xx}
    c_dev = {"gy": yy * 2 + 1 - cc}
    y1_dev = {"gy": (b1 * 2 + 1 - b0) * 2 + cc}
    y2_dev = {"gy": ((1 - b1) * 2 + b0) * 2 + cc}
    y3_dev = {"gy": ((1 - b1) * 2 + 1 - b0) * 2 + cc}
    zp, zm = {"gz": (z + 1) % 8}, {"gz": (z + 7) % 8}

    barrier = pltpu.get_barrier_semaphore()
    partners = [{"gx": (gx + k) % 8} for k in range(1, 8)]
    partners += [{"gz": (z + k) % 8} for k in range(1, 8)]
    partners += [c_dev, y1_dev, y2_dev, y3_dev]
    for dev in partners:
        pl.semaphore_signal(barrier, inc=1, device_id=dev, device_id_type=MESH)

    slots = {}
    kinds = {}

    def rc(src, dst, name, dev):
        kind = name[0] + str(name[2] % 2) if name[0] == "w" else name[0]
        group = name[: TOGETHER[name[0]]] if name[0] in TOGETHER else name
        k = kinds.setdefault(kind, len(kinds))
        slot = slots.setdefault(group, len(slots))
        return pltpu.make_async_remote_copy(
            src_ref=src, dst_ref=dst, send_sem=s_all.at[k], recv_sem=r_all.at[slot],
            device_id=dev, device_id_type=MESH,
        )

    def send(src, dst, name, dev):
        rc(src, dst, name, dev).start()

    waited = set()

    def arrived(ref, name):
        if name not in waited:
            waited.add(name)
            rc(ref, ref, name, c_dev).wait_recv()

    def zrows(i):
        return pl.ds(pl.multiple_of(i * 96, 32), 96)

    own = zrows(z)
    local = [
        pltpu.make_async_copy(x_in, xg.at[0, 0, own, :], l_sem.at[0]),
        pltpu.make_async_copy(g_in, xg.at[1, 0, own, :], l_sem.at[1]),
        pltpu.make_async_copy(win, wi.at[0], l_sem.at[2]),
        pltpu.make_async_copy(wout, wo.at[0], l_sem.at[3]),
    ]
    for copy in local:
        copy.start()
    pl.semaphore_wait(barrier, len(partners))

    hops = ((4, 3), (3, 4))

    def zref(r, a, d, s):
        begun = (z + 8 - s) % 8 if d == 0 else (z + s) % 8
        return xg.at[a, r, zrows(begun), :]

    def zsend(r, a, d, s):
        ref = zref(r, a, d, s - 1)
        src = (x_in, g_in)[a] if r == 0 and s == 1 else ref
        send(src, ref, ("z", r, a, d, s), zp if d == 0 else zm)

    def do_z(r, a, d, s):
        arrived(zref(r, a, d, s), ("z", r, a, d, s))
        if s < hops[a][d]:
            zsend(r, a, d, s + 1)

    def do_hs(a):
        arrived(xg.at[a, 1, own, :], ("h", a))
        for d in range(2):
            zsend(1, a, d, 1)

    def do_start():
        for a in range(2):
            send((x_in, g_in)[a], xg.at[a, 1, own, :], ("h", a), h_dev)
            for d in range(2):
                zsend(0, a, d, 1)

    def piece(b):
        return pl.ds(b * CH, CH)

    def do_wstart(b):
        send(win.at[:, piece(b)], wi.at[3, :, piece(b)], ("w", b, 0), xp)
        send(win.at[:, piece(b)], wi.at[1, :, piece(b)], ("w", b, 2), xm)
        send(wout.at[piece(b), :], wo.at[3, piece(b), :], ("w", b, 1), xp)
        send(wout.at[piece(b), :], wo.at[1, piece(b), :], ("w", b, 3), xm)

    def do_wf(b, i):
        if i == 0:
            arrived(wi.at[3, :, piece(b)], ("w", b, 0))
            send(wi.at[3, :, piece(b)], wi.at[2, :, piece(b)], ("w", b, 4), xp)
        else:
            arrived(wo.at[1, piece(b), :], ("w", b, 3))
            send(wo.at[1, piece(b), :], wo.at[2, piece(b), :], ("w", b, 5), xm)

    own_w = []

    def w_here(s, b):
        if s == 1:
            arrived(wi.at[1, :, piece(b)], ("w", b, 2))
        elif s == 2:
            arrived(wi.at[2, :, piece(b)], ("w", b, 4))
            arrived(wo.at[2, piece(b), :], ("w", b, 5))
        elif s == 3:
            arrived(wo.at[3, piece(b), :], ("w", b, 1))

    def rows(i, n):
        return pl.ds(pl.multiple_of(i * n, n), n)

    def do_a(s, b, r):
        c = index(s, b, r)
        if not own_w:
            own_w.append(True)
            for copy in local:
                copy.wait()
        w_here(s, b)
        pre = dot(wi[s, :, b * CH : (b + 1) * CH], xg[0, r], 0, 0)
        back = dot(wo[s, b * CH : (b + 1) * CH, :], xg[1, r], 1, 0)
        for k, val in enumerate((pre, back)):
            pown[c, k] = val
            psend[c, k] = val.astype(BF)
        send(psend.at[c, :, rows(1 - cc, CH // 2), :], crecv.at[c], ("c", c), c_dev)

    def do_b(s, b, r):
        c = index(s, b, r)
        arrived(crecv.at[c], ("c", c))
        total = pown[c, :, rows(cc, CH // 2), :] + crecv[c].astype(F32)
        pown[c, :, : CH // 2, :] = total
        ysend[c] = total.astype(BF)
        send(ysend.at[c, :, rows(1 - b0, CH // 4), :], yrecv.at[c], ("y", c), y1_dev)

    def do_b2(s, b, r):
        c = index(s, b, r)
        arrived(yrecv.at[c], ("y", c))
        total = pown[c, :, rows(b0, CH // 4), :] + yrecv[c].astype(F32)
        pown[c, :, : CH // 4, :] = total
        y2send[c] = total.astype(BF)
        send(y2send.at[c, :, rows(1 - b1, CH // 8), :], y2recv.at[c], ("y2", c), y2_dev)

    def hrows(p0, p1):
        return rows(cc * 4 + p0 * 2 + p1, CH // 8)

    def do_c(s, b, r):
        c = index(s, b, r)
        arrived(y2recv.at[c], ("y2", c))
        total = pown[c, :, rows(b1, CH // 8), :] + y2recv[c].astype(F32)
        ht[c, hrows(b0, b1), :] = (total[1] * gelu_slope(total[0])).astype(BF)
        ref = ht.at[c, hrows(b0, b1), :]
        for k, dev in ((1, y1_dev), (2, y2_dev), (3, y3_dev)):
            send(ref, ref, ("ah", c, k), dev)

    def do_d(s, b, r):
        c = index(s, b, r)
        arrived(ht.at[c, : 3 * CH // 8, :], ("ah", c))
        ref = ht.at[c, rows(cc, CH // 2), :]
        send(ref, ref, ("ac", c), c_dev)

    first = [True, True]

    def do_e(s, b, r):
        c = index(s, b, r)
        arrived(ht.at[c, rows(1 - cc, CH // 2), :], ("ac", c))
        val = dot(wi[s, :, b * CH : (b + 1) * CH], ht[c], 1, 0)
        dxacc[r] = val if first[r] else dxacc[r] + val
        first[r] = False

    def do_dx(r):
        dxs[r] = dxacc[r].astype(BF)
        for k in (4, 3, 5, 2, 6, 1, 7):
            to = (z + k) % 8
            send(dxs.at[r, zrows(to), :], dxr.at[r, k - 1], ("dx", r, k), {"gz": to})

    def do_dw(s, b):
        dw = dot(xg[0, 0], ht[index(s, b, 0)], 1, 1) + dot(xg[0, 1], ht[index(s, b, 1)], 1, 1)
        if s == 0:
            dwf0[b] = dw
        elif s == 1:
            dwf[b, 0] = dw[:384]
            put_dw(b, 2, dw[384:], xp)
        elif s == 2:
            put_dw(b, 0, dw[:384], xp)
            put_dw(b, 1, dw[384:], xm)
        else:
            dwf[b, 1] = dw[384:]
            put_dw(b, 3, dw[:384], xm)

    def put_dw(b, i, val, dev):
        dws[b, i] = val.astype(BF)
        send(dws.at[b, i], dwr.at[b, i], ("dw", b, i), dev)

    def do_add(b, i):
        arrived(dwr.at[b, i], ("dw", b, i))
        put_dw(b, 4 + i, dwf[b, i] + dwr[b, i].astype(F32), xm if i else xp)

    def do_own(b):
        for i in (2, 3, 4, 5):
            arrived(dwr.at[b, i], ("dw", b, i))
        low = dwf0[b, :384] + dwr[b, 3].astype(F32) + dwr[b, 4].astype(F32)
        high = dwf0[b, 384:] + dwr[b, 2].astype(F32) + dwr[b, 5].astype(F32)
        dw_out[:384, b * CH : (b + 1) * CH] = low.astype(BF)
        dw_out[384:, b * CH : (b + 1) * CH] = high.astype(BF)

    scaled = {}

    def do_sq():
        wf = dw_out[...].astype(F32)
        sqs[...] = jnp.broadcast_to(jnp.sum(wf * wf), (8, 128))
        for k in range(1, 8):
            send(sqs, sqr.at[k - 1], ("sq", k), {"gx": (gx + k) % 8})
        scaled["w"] = (wf * UP).astype(BF)

    x1, x2, x3 = (xx + 1) % 4, (xx + 2) % 4, (xx + 3) % 4
    width = 768 // NP

    def put_g(p, i, val, dev):
        gsend[p, i] = val.astype(BF)
        send(gsend.at[p, i], grecv.at[p, i], ("g", p, i), dev)

    def do_g(p):
        ws = scaled["w"]
        gbuf[p] = dot(ws, ws[p * width : (p + 1) * width], 1, 1).reshape(2, 4, 96, width)
        put_g(p, 0, gbuf[p, 0, x2], xp)
        put_g(p, 1, gbuf[p, 1, x2], xm)

    def do_g2(p):
        put_g(p, 2, gbuf[p, 1, x1], xp)
        put_g(p, 3, gbuf[p, 0, x3], xm)

    def do_ga(p, i):
        arrived(grecv.at[p, i], ("g", p, i))
        mine = gbuf[p, 1, x3] if i else gbuf[p, 0, x1]
        put_g(p, 4 + i, mine + grecv[p, i].astype(F32), xm if i else xp)

    def do_go(p):
        for i in (2, 3, 4, 5):
            arrived(grecv.at[p, i], ("g", p, i))
        gbuf[p, 0, xx] = gbuf[p, 0, xx] + grecv[p, 3].astype(F32) + grecv[p, 4].astype(F32)
        gbuf[p, 1, xx] = gbuf[p, 1, xx] + grecv[p, 2].astype(F32) + grecv[p, 5].astype(F32)
        ghs[p] = gbuf[p, 1 - hi, xx].astype(BF)
        send(ghs.at[p], ghr.at[p], ("gh", p), h_dev)

    def do_gf(p):
        if "factor" not in scaled:
            sq = sqs[...]
            arrived(sqr, ("sq",))
            for k in range(1, 8):
                sq = sq + sqr[k - 1]
            scaled["factor"] = DOWN / (jnp.sqrt(sq[:1, :1]) + 1e-07)
        factor = scaled["factor"]
        arrived(ghr.at[p], ("gh", p))
        val = (gbuf[p, hi, xx] + ghr[p].astype(F32)) * factor * factor * 768.0
        gram_out[:, p * width : (p + 1) * width] = val

    def do_dxs(r):
        total = dxacc[r, own, :]
        arrived(dxr.at[r], ("dx", r))
        for k in range(1, 8):
            total = total + dxr[r, k - 1].astype(F32)
        if r == 1:
            dxh[...] = total.astype(BF)
            send(dxh, dxhr, ("dxh",), h_dev)
        else:
            dxo[...] = total

    def do_dxf():
        arrived(dxhr, ("dxh",))
        dx_out[...] = (dxo[...] + dxhr[...].astype(F32)).astype(BF)

    steps = {
        "start": do_start, "wstart": do_wstart, "hs": do_hs, "z": do_z, "wf": do_wf,
        "A": do_a, "B": do_b, "B2": do_b2, "C": do_c, "D": do_d, "E": do_e, "dw": do_dw, "add": do_add, "own": do_own,
        "sq": do_sq, "g": do_g, "g2": do_g2, "ga": do_ga, "go": do_go, "gf": do_gf,
        "dx": do_dx, "dxs": do_dxs, "dxf": do_dxf,
    }
    for step in SCHEDULE:
        steps[step[0]](*step[1:])

    totals = {
        "h": xg.at[:, 0, :96, :], "z": xg.at[:, :, :672, :], "w0": wi.at[:3], "w1": wo.at[:3],
        "c": crecv, "y": yrecv, "y2": y2recv, "ah": ht.at[:, : 3 * CH // 8, :], "ac": ht.at[:, : CH // 2, :],
        "dw": dwr, "dx": dxr, "sq": sqr, "g": grecv, "gh": ghr, "dxh": dxhr,
    }
    for kind, ref in totals.items():
        k = kinds[kind]
        pltpu.make_async_remote_copy(
            src_ref=ref, dst_ref=ref, send_sem=s_all.at[k], recv_sem=r_all.at[0],
            device_id=c_dev, device_id_type=MESH,
        ).wait_send()


def body(inputs, out_grad, w_in, w_out):
    vmem = pl.BlockSpec(memory_space=pltpu.VMEM)
    hbm = pl.BlockSpec(memory_space=pl.ANY)
    dma = pltpu.SemaphoreType.DMA
    n = 8 * NH
    width = 768 // NP
    dx_t, weight_grad, gram = pl.pallas_call(
        kernel,
        out_shape=(
            jax.ShapeDtypeStruct((96, 256), BF),
            jax.ShapeDtypeStruct((768, 256), BF),
            jax.ShapeDtypeStruct((96, 768), F32),
        ),
        in_specs=[hbm] * 4,
        out_specs=(vmem,) * 3,
        scratch_shapes=[
            pltpu.VMEM((2, 2, 768, 256), BF),
            pltpu.VMEM((4, 768, 256), BF),
            pltpu.VMEM((4, 256, 768), BF),
            pltpu.VMEM((n, 2, CH, 256), BF),
            pltpu.VMEM((n, 2, CH, 256), F32),
            pltpu.VMEM((n, 2, CH // 2, 256), BF),
            pltpu.VMEM((n, 2, CH // 2, 256), BF),
            pltpu.VMEM((n, 2, CH // 4, 256), BF),
            pltpu.VMEM((n, 2, CH // 4, 256), BF),
            pltpu.VMEM((n, 2, CH // 8, 256), BF),
            pltpu.VMEM((n, CH, 256), BF),
            pltpu.VMEM((2, 768, 256), F32),
            pltpu.VMEM((96, 256), F32),
            pltpu.VMEM((2, 768, 256), BF),
            pltpu.VMEM((2, 7, 96, 256), BF),
            pltpu.VMEM((96, 256), BF),
            pltpu.VMEM((96, 256), BF),
            pltpu.VMEM((NH, 2, 384, CH), F32),
            pltpu.VMEM((NH, 768, CH), F32),
            pltpu.VMEM((NH, 6, 384, CH), BF),
            pltpu.VMEM((NH, 6, 384, CH), BF),
            pltpu.VMEM((NP, 2, 4, 96, width), F32),
            pltpu.VMEM((NP, 6, 96, width), BF),
            pltpu.VMEM((NP, 6, 96, width), BF),
            pltpu.VMEM((NP, 96, width), BF),
            pltpu.VMEM((NP, 96, width), BF),
            pltpu.VMEM((8, 128), F32),
            pltpu.VMEM((7, 8, 128), F32),
            dma((4,)), dma((KINDS,)), dma((SLOTS,)),
        ],
        compiler_params=pltpu.CompilerParams(
            collective_id=0, has_side_effects=True, vmem_limit_bytes=60 * 1024 * 1024
        ),
        cost_estimate=pl.CostEstimate(
            flops=3_600_000_000, bytes_accessed=4_000_000, transcendentals=131072
        ),
    )(inputs.T, out_grad.T, w_in, w_out)
    return (dx_t.T, weight_grad, gram[None])


def solution(mesh):
    placed = (
        P("gx", ("gy", "gz")),
        P("gx", ("gy", "gz")),
        P("gy", ("gx", "gz")),
        P(("gx", "gz"), "gy"),
    )
    return jax.shard_map(
        body,
        mesh=mesh,
        in_specs=placed,
        out_specs=(P("gx", ("gy", "gz")), P("gy", ("gx", "gz")), P("gz", ("gy", "gx"), None)),
        check_vma=False,
    )
```

time: 110 us -> 98.2 us (0.89)
  Pallas kernels: 104 us -> 93.4 us
  local copies, waits for them, and re-layouts: 5.11 us -> 3.95 us
    pallas_call x1, Pallas kernels: 104 us -> 93.4 us  [body(): pl.pallas_call(kernel, out_shape=(jax.ShapeDtypeStruct((96, 256), BF), ja...]
    unnamed x11 -> x5, local copies, waits for them, and re-layouts: 5.11 us -> 3.95 us
where the time goes in v3:
time: 98.2 us; the launch traced here: 98 us
  Pallas kernels  93.4 us (95%)
  local copies, waits for them, and re-layouts  3.95 us (4%)
    pallas_call x1, Pallas kernels, body(): pl.pallas_call(kernel, out_shape=(jax.ShapeDtypeStruct((96, 256), BF), ja...  93.4 us
    unnamed x5, local copies, waits for them, and re-layouts  3.95 us

profile of v3, /device:TPU:1, one launch (start us, length us, event | category | flops | bytes accessed | tf_op | source)
XLA Modules:
  0.0 98.0 jit_solution(17904131865033500567)
XLA Ops:
  0.6 93.4 %shard_map.67 = (bf16[96,256]{1,0:T(8,128)(2,1)}, bf16[768,256]{1,0:T(8,128)(2,1)}, f32[96,768]{1,0:T(8,128)}) custom-call(bf16[96,256]{1,0:T(8,128)(2,1)} %bitcast.6, bf16[96,256]{1,0:T(8,128)(2,1)} %bitcast.7, bf16[768,256]{1,0:T(8,128)(2,1)} %win.1, bf16[256,768]{1,0:T(8,128)(2,1)} %wout.1), custom_call_target="tpu_custom_call" | custom-call | flops 3600000000 | bytes 4000000 | tf_op jit(solution)/shard_map/pallas_call | solution.py:376
  94.1 1.4 %copy.10 = bf16[256,96]{0,1:T(8,128)(2,1)} copy(bf16[256,96]{0,1:T(8,128)(2,1)} %bitcast.5) | data formatting | bytes 98304
  95.5 0.0 copy-start
  95.5 1.8 %copy.11 = bf16[768,256]{1,0:T(8,128)(2,1)} copy(bf16[768,256]{1,0:T(8,128)(2,1)} %get-tuple-element.13) | data formatting | bytes 786432
  97.3 0.0 copy-done
  97.3 0.7 copy.12
Async XLA Ops:
  95.5 1.8 %copy-start = (f32[96,768]{1,0:T(8,128)S(1)}, f32[96,768]{1,0:T(8,128)}, u32[]{:S(2)}) copy-start(f32[96,768]{1,0:T(8,128)} %get-tuple-element.8) | copy-start | bytes 884740

commit v4 on v3

--- a/solution.py
+++ b/solution.py
@@ -13,37 +13,42 @@
 DOWN = float(2.0**-30)
 NH = 2
 CH = 256 // NH
-NP = 3
+NP = 6
 KINDS = 16
-SLOTS = 160
+ZT = 1
+SLOTS = 156
 TOGETHER = {"ah": 2, "dx": 2, "sq": 1}
+LATE = (2, 3, 4, 5)
 
 SCHEDULE = [
-    ("start",), ("wstart", 0), ("z", 0, 1, 1, 1), ("z", 0, 0, 0, 1), ("wstart", 1), ("z", 0, 1, 0, 1), ("hs", 0),
-    ("z", 0, 0, 1, 1), ("z", 0, 1, 1, 2), ("z", 0, 0, 0, 2), ("hs", 1), ("z", 0, 0, 1, 2), ("z", 1, 0, 0, 1),
-    ("z", 0, 0, 0, 3), ("z", 0, 1, 0, 2), ("z", 0, 1, 1, 3), ("z", 1, 1, 1, 1), ("wf", 0, 0), ("z", 1, 0, 1, 1),
-    ("z", 1, 0, 0, 2), ("z", 0, 0, 0, 4), ("z", 0, 0, 1, 3), ("wf", 0, 1), ("z", 1, 1, 1, 2), ("z", 0, 1, 0, 3),
-    ("z", 0, 1, 1, 4), ("A", 3, 0, 0), ("z", 1, 1, 0, 1), ("A", 1, 0, 0), ("z", 1, 0, 1, 2), ("B", 3, 0, 0),
-    ("z", 1, 0, 0, 3), ("B", 1, 0, 0), ("wf", 1, 0), ("A", 0, 1, 0), ("A", 3, 1, 0), ("wf", 1, 1), ("z", 1, 1, 1, 3),
-    ("z", 1, 1, 0, 2), ("B", 3, 1, 0), ("z", 1, 0, 0, 4), ("A", 1, 1, 0), ("A", 0, 0, 0), ("z", 1, 0, 1, 3),
-    ("B2", 3, 0, 0), ("B", 1, 1, 0), ("B", 0, 1, 0), ("B2", 1, 0, 0), ("z", 1, 1, 1, 4), ("A", 2, 0, 0),
-    ("B2", 3, 1, 0), ("z", 1, 1, 0, 3), ("A", 1, 0, 1), ("B", 2, 0, 0), ("A", 2, 0, 1), ("B", 1, 0, 1),
-    ("A", 3, 0, 1), ("B", 2, 0, 1), ("B", 3, 0, 1), ("B2", 1, 1, 0), ("A", 3, 1, 1), ("C", 3, 0, 0), ("A", 2, 1, 1),
-    ("B2", 2, 0, 0), ("A", 2, 1, 0), ("C", 1, 0, 0), ("A", 1, 1, 1), ("B", 2, 1, 1), ("B2", 2, 0, 1), ("B", 2, 1, 0),
-    ("B2", 3, 0, 1), ("A", 0, 0, 1), ("A", 0, 1, 1), ("B", 1, 1, 1), ("B2", 1, 0, 1), ("B", 3, 1, 1), ("C", 2, 0, 0),
-    ("B2", 2, 1, 1), ("D", 3, 0, 0), ("C", 2, 0, 1), ("B2", 2, 1, 0), ("C", 3, 0, 1), ("C", 1, 0, 1), ("B", 0, 0, 1),
-    ("B", 0, 1, 1), ("B2", 3, 1, 1), ("C", 3, 1, 0), ("C", 2, 1, 1), ("D", 2, 0, 0), ("D", 1, 0, 0), ("D", 2, 0, 1),
-    ("C", 2, 1, 0), ("E", 1, 0, 0), ("E", 2, 0, 0), ("B2", 1, 1, 1), ("B2", 0, 0, 1), ("D", 3, 0, 1), ("E", 2, 0, 1),
-    ("dw", 2, 0), ("B2", 0, 1, 1), ("D", 1, 0, 1), ("C", 1, 1, 0), ("C", 3, 1, 1), ("E", 3, 0, 0), ("B2", 0, 1, 0),
-    ("E", 3, 0, 1), ("E", 1, 0, 1), ("dw", 3, 0), ("B", 0, 0, 0), ("dw", 1, 0), ("C", 1, 1, 1), ("D", 2, 1, 0),
-    ("D", 2, 1, 1), ("C", 0, 0, 1), ("E", 2, 1, 0), ("E", 2, 1, 1), ("dw", 2, 1), ("C", 0, 1, 1), ("D", 3, 1, 0),
-    ("add", 0, 1), ("B2", 0, 0, 0), ("E", 3, 1, 0), ("add", 0, 0), ("C", 0, 1, 0), ("D", 3, 1, 1), ("D", 1, 1, 0),
-    ("D", 1, 1, 1), ("E", 3, 1, 1), ("dw", 3, 1), ("E", 1, 1, 0), ("E", 1, 1, 1), ("dw", 1, 1), ("D", 0, 0, 1),
-    ("C", 0, 0, 0), ("D", 0, 1, 1), ("add", 1, 1), ("add", 1, 0), ("E", 0, 0, 1), ("E", 0, 1, 1), ("dx", 1),
-    ("D", 0, 1, 0), ("E", 0, 1, 0), ("dw", 0, 1), ("D", 0, 0, 0), ("E", 0, 0, 0), ("dw", 0, 0), ("own", 0),
-    ("own", 1), ("sq",), ("g", 0), ("g", 2), ("g", 1), ("g2", 0), ("dx", 0), ("ga", 0, 0), ("ga", 0, 1), ("g2", 1),
-    ("dxs", 1), ("ga", 1, 1), ("ga", 2, 1), ("ga", 1, 0), ("ga", 2, 0), ("go", 0), ("g2", 2), ("go", 1), ("go", 2),
-    ("dxs", 0), ("gf", 0), ("gf", 1), ("dxf",), ("gf", 2),
+    ("start",), ("wstart", 0), ("z", 0, 0, 0, 1, 0), ("wstart", 1), ("z", 0, 0, 1, 1, 0), ("z", 0, 1, 0, 1, 0),
+    ("z", 0, 1, 1, 1, 0), ("hs", 0, 0), ("z", 0, 0, 0, 2, 0), ("hs", 1, 0), ("z", 0, 1, 1, 2, 0),
+    ("z", 0, 0, 1, 2, 0), ("z", 1, 0, 0, 1, 0), ("z", 0, 0, 0, 3, 0), ("z", 1, 1, 1, 1, 0), ("z", 0, 1, 0, 2, 0),
+    ("z", 1, 1, 0, 1, 0), ("wf", 0, 0), ("z", 0, 1, 1, 3, 0), ("z", 1, 0, 0, 2, 0), ("z", 1, 0, 1, 1, 0),
+    ("z", 0, 0, 0, 4, 0), ("wf", 1, 0), ("z", 1, 1, 1, 2, 0), ("z", 0, 1, 0, 3, 0), ("z", 0, 0, 1, 3, 0),
+    ("wf", 0, 1), ("z", 0, 1, 1, 4, 0), ("A", 1, 0, 0), ("A", 3, 0, 0), ("A", 0, 1, 0), ("B", 1, 0, 0),
+    ("z", 1, 0, 1, 2, 0), ("z", 1, 1, 0, 2, 0), ("B", 3, 0, 0), ("z", 1, 0, 0, 3, 0), ("B", 0, 1, 0), ("wf", 1, 1),
+    ("A", 1, 1, 0), ("z", 1, 1, 1, 3, 0), ("A", 3, 1, 0), ("B", 1, 1, 0), ("B2", 3, 0, 0), ("z", 1, 0, 1, 3, 0),
+    ("B2", 1, 0, 0), ("B", 3, 1, 0), ("B2", 0, 1, 0), ("z", 1, 0, 0, 4, 0), ("A", 2, 0, 0), ("z", 1, 1, 0, 3, 0),
+    ("z", 1, 1, 1, 4, 0), ("A", 2, 0, 1), ("B2", 1, 1, 0), ("B", 2, 0, 0), ("A", 3, 0, 1), ("B", 2, 0, 1),
+    ("A", 1, 0, 1), ("B", 3, 0, 1), ("A", 1, 1, 1), ("B2", 3, 1, 0), ("B", 1, 0, 1), ("C", 3, 0, 0), ("A", 0, 1, 1),
+    ("A", 2, 1, 0), ("B2", 2, 0, 0), ("A", 2, 1, 1), ("B2", 2, 0, 1), ("B", 2, 1, 0), ("A", 0, 0, 1), ("B", 2, 1, 1),
+    ("B2", 3, 0, 1), ("B2", 1, 0, 1), ("B", 1, 1, 1), ("A", 3, 1, 1), ("C", 1, 0, 0), ("C", 2, 0, 0), ("B", 3, 1, 1),
+    ("B2", 2, 1, 0), ("B2", 2, 1, 1), ("C", 2, 0, 1), ("C", 3, 0, 1), ("B", 0, 1, 1), ("D", 3, 0, 0), ("B", 0, 0, 1),
+    ("C", 1, 0, 1), ("B2", 1, 1, 1), ("A", 0, 0, 0), ("B2", 3, 1, 1), ("E", 3, 0, 0), ("C", 2, 1, 0), ("D", 1, 0, 0),
+    ("D", 2, 0, 0), ("C", 2, 1, 1), ("E", 1, 0, 0), ("B2", 0, 1, 1), ("D", 2, 0, 1), ("E", 2, 0, 0), ("B2", 0, 0, 1),
+    ("C", 1, 1, 0), ("D", 3, 0, 1), ("E", 2, 0, 1), ("dw", 2, 0), ("B", 0, 0, 0), ("C", 3, 1, 0), ("E", 3, 0, 1),
+    ("D", 1, 0, 1), ("C", 3, 1, 1), ("C", 1, 1, 1), ("dw", 3, 0), ("E", 1, 0, 1), ("dw", 1, 0), ("D", 2, 1, 1),
+    ("C", 0, 1, 1), ("D", 2, 1, 0), ("C", 0, 0, 1), ("E", 2, 1, 1), ("B2", 0, 0, 0), ("E", 2, 1, 0), ("dw", 2, 1),
+    ("C", 0, 1, 0), ("D", 1, 1, 0), ("add", 0, 1), ("D", 3, 1, 0), ("D", 3, 1, 1), ("add", 0, 0), ("D", 1, 1, 1),
+    ("E", 1, 1, 0), ("E", 3, 1, 0), ("E", 3, 1, 1), ("D", 0, 1, 1), ("dw", 3, 1), ("E", 1, 1, 1), ("D", 0, 0, 1),
+    ("dw", 1, 1), ("C", 0, 0, 0), ("E", 0, 1, 1), ("E", 0, 0, 1), ("dx", 1), ("D", 0, 1, 0), ("add", 1, 0),
+    ("add", 1, 1), ("E", 0, 1, 0), ("dw", 0, 1), ("D", 0, 0, 0), ("E", 0, 0, 0), ("dw", 0, 0), ("own", 0), ("own", 1),
+    ("sq",), ("g", 5), ("g", 0), ("g", 1), ("g", 3), ("sq2",), ("g2", 5), ("g", 4), ("dx", 0), ("g", 2), ("ga", 5, 0),
+    ("ga", 5, 1), ("g2", 0), ("ga", 0, 0), ("ga", 0, 1), ("ga", 1, 1), ("g2", 1), ("dxs", 1), ("ga", 1, 0),
+    ("ga", 4, 0), ("g2", 4), ("ga", 4, 1), ("ga", 3, 0), ("ga", 3, 1), ("go", 5), ("g2", 3), ("ga", 2, 0),
+    ("ga", 2, 1), ("go", 0), ("g2", 2), ("go", 1), ("go", 4), ("go", 3), ("go", 2), ("gf", 0), ("gf", 5), ("gf", 1),
+    ("gf", 4), ("gf", 3), ("dxs", 0), ("dxf",), ("gf", 2),
 ]
 
 
@@ -97,6 +102,8 @@
     def rc(src, dst, name, dev):
         kind = name[0] + str(name[2] % 2) if name[0] == "w" else name[0]
         group = name[: TOGETHER[name[0]]] if name[0] in TOGETHER else name
+        if name[0] in ("dw", "g") and name[2] in LATE:
+            group = name[:2]
         k = kinds.setdefault(kind, len(kinds))
         slot = slots.setdefault(group, len(slots))
         return pltpu.make_async_remote_copy(
@@ -130,30 +137,36 @@
 
     hops = ((4, 3), (3, 4))
 
-    def zref(r, a, d, s):
+    def lanes(t):
+        return pl.ds(t * (256 // ZT), 256 // ZT)
+
+    def zref(r, a, d, s, t):
         begun = (z + 8 - s) % 8 if d == 0 else (z + s) % 8
-        return xg.at[a, r, zrows(begun), :]
-
-    def zsend(r, a, d, s):
-        ref = zref(r, a, d, s - 1)
-        src = (x_in, g_in)[a] if r == 0 and s == 1 else ref
-        send(src, ref, ("z", r, a, d, s), zp if d == 0 else zm)
-
-    def do_z(r, a, d, s):
-        arrived(zref(r, a, d, s), ("z", r, a, d, s))
+        return xg.at[a, r, zrows(begun), lanes(t)]
+
+    def zsend(r, a, d, s, t):
+        ref = zref(r, a, d, s - 1, t)
+        src = (x_in, g_in)[a].at[:, lanes(t)] if r == 0 and s == 1 else ref
+        send(src, ref, ("z", r, a, d, s, t), zp if d == 0 else zm)
+
+    def do_z(r, a, d, s, t):
+        arrived(zref(r, a, d, s, t), ("z", r, a, d, s, t))
         if s < hops[a][d]:
-            zsend(r, a, d, s + 1)
-
-    def do_hs(a):
-        arrived(xg.at[a, 1, own, :], ("h", a))
+            zsend(r, a, d, s + 1, t)
+
+    def do_hs(a, t):
+        arrived(xg.at[a, 1, own, lanes(t)], ("h", a, t))
         for d in range(2):
-            zsend(1, a, d, 1)
+            zsend(1, a, d, 1, t)
 
     def do_start():
         for a in range(2):
-            send((x_in, g_in)[a], xg.at[a, 1, own, :], ("h", a), h_dev)
-            for d in range(2):
-                zsend(0, a, d, 1)
+            for t in range(ZT):
+                send((x_in, g_in)[a].at[:, lanes(t)], xg.at[a, 1, own, lanes(t)], ("h", a, t), h_dev)
+        for a in range(2):
+            for t in range(ZT):
+                for d in range(2):
+                    zsend(0, a, d, 1, t)
 
     def piece(b):
         return pl.ds(b * CH, CH)
@@ -272,8 +285,7 @@
         put_dw(b, 4 + i, dwf[b, i] + dwr[b, i].astype(F32), xm if i else xp)
 
     def do_own(b):
-        for i in (2, 3, 4, 5):
-            arrived(dwr.at[b, i], ("dw", b, i))
+        arrived(dwr.at[b, 2:], ("dw", b, 2))
         low = dwf0[b, :384] + dwr[b, 3].astype(F32) + dwr[b, 4].astype(F32)
         high = dwf0[b, 384:] + dwr[b, 2].astype(F32) + dwr[b, 5].astype(F32)
         dw_out[:384, b * CH : (b + 1) * CH] = low.astype(BF)
@@ -282,11 +294,13 @@
     scaled = {}
 
     def do_sq():
+        scaled["w"] = (dw_out[...].astype(F32) * UP).astype(BF)
+
+    def do_sq2():
         wf = dw_out[...].astype(F32)
         sqs[...] = jnp.broadcast_to(jnp.sum(wf * wf), (8, 128))
         for k in range(1, 8):
             send(sqs, sqr.at[k - 1], ("sq", k), {"gx": (gx + k) % 8})
-        scaled["w"] = (wf * UP).astype(BF)
 
     x1, x2, x3 = (xx + 1) % 4, (xx + 2) % 4, (xx + 3) % 4
     width = 768 // NP
@@ -311,8 +325,7 @@
         put_g(p, 4 + i, mine + grecv[p, i].astype(F32), xm if i else xp)
 
     def do_go(p):
-        for i in (2, 3, 4, 5):
-            arrived(grecv.at[p, i], ("g", p, i))
+        arrived(grecv.at[p, 2:], ("g", p, 2))
         gbuf[p, 0, xx] = gbuf[p, 0, xx] + grecv[p, 3].astype(F32) + grecv[p, 4].astype(F32)
         gbuf[p, 1, xx] = gbuf[p, 1, xx] + grecv[p, 2].astype(F32) + grecv[p, 5].astype(F32)
         ghs[p] = gbuf[p, 1 - hi, xx].astype(BF)
@@ -348,7 +361,7 @@
     steps = {
         "start": do_start, "wstart": do_wstart, "hs": do_hs, "z": do_z, "wf": do_wf,
         "A": do_a, "B": do_b, "B2": do_b2, "C": do_c, "D": do_d, "E": do_e, "dw": do_dw, "add": do_add, "own": do_own,
-        "sq": do_sq, "g": do_g, "g2": do_g2, "ga": do_ga, "go": do_go, "gf": do_gf,
+        "sq": do_sq, "sq2": do_sq2, "g": do_g, "g2": do_g2, "ga": do_ga, "go": do_go, "gf": do_gf,
         "dx": do_dx, "dxs": do_dxs, "dxf": do_dxf,
     }
     for step in SCHEDULE:
@@ -367,19 +380,33 @@
         ).wait_send()
 
 
+def hand_on(*refs):
+    sem = refs[-1]
+    copies = [pltpu.make_async_copy(refs[i], refs[6 + i], sem.at[i]) for i in range(3)]
+    copies += [pltpu.make_async_copy(refs[6 + i], refs[3 + i], sem.at[3 + i]) for i in range(3)]
+    for copy in copies[:3]:
+        copy.start()
+    for i in range(3):
+        copies[i].wait()
+        copies[3 + i].start()
+    for copy in copies[3:]:
+        copy.wait()
+
+
 def body(inputs, out_grad, w_in, w_out):
     vmem = pl.BlockSpec(memory_space=pltpu.VMEM)
     hbm = pl.BlockSpec(memory_space=pl.ANY)
     dma = pltpu.SemaphoreType.DMA
     n = 8 * NH
     width = 768 // NP
-    dx_t, weight_grad, gram = pl.pallas_call(
+    out_shape = (
+        jax.ShapeDtypeStruct((96, 256), BF),
+        jax.ShapeDtypeStruct((768, 256), BF),
+        jax.ShapeDtypeStruct((96, 768), F32),
+    )
+    results = pl.pallas_call(
         kernel,
-        out_shape=(
-            jax.ShapeDtypeStruct((96, 256), BF),
-            jax.ShapeDtypeStruct((768, 256), BF),
-            jax.ShapeDtypeStruct((96, 768), F32),
-        ),
+        out_shape=out_shape,
         in_specs=[hbm] * 4,
         out_specs=(vmem,) * 3,
         scratch_shapes=[
@@ -420,6 +447,13 @@
             flops=3_600_000_000, bytes_accessed=4_000_000, transcendentals=131072
         ),
     )(inputs.T, out_grad.T, w_in, w_out)
+    dx_t, weight_grad, gram = pl.pallas_call(
+        hand_on,
+        out_shape=out_shape,
+        in_specs=[hbm] * 3,
+        out_specs=(hbm,) * 3,
+        scratch_shapes=[pltpu.VMEM(v.shape, v.dtype) for v in out_shape] + [dma((6,))],
+    )(*results)
     return (dx_t.T, weight_grad, gram[None])
 
 

time: 98.2 us -> 94.1 us (0.958)
  local copies, waits for them, and re-layouts: 3.95 us -> 0 us
    unnamed x5 -> x0, local copies, waits for them, and re-layouts: 3.95 us -> none
    pallas_call x1 -> x2, Pallas kernels: 93.4 us -> 92.9 us  [the longest x1 91 us: body(): pl.pallas_call(kernel, out_shape=out_shape, in_specs=[hbm] * 4, out_specs...]
where the time goes in v4:
time: 94.1 us; the launch traced here: 93.5 us
  Pallas kernels  92.9 us (99%)
    pallas_call x1, Pallas kernels, body(): pl.pallas_call(kernel, out_shape=out_shape, in_specs=[hbm] * 4, out_specs...  91 us
    pallas_call x1, Pallas kernels, body(): pl.pallas_call(hand_on, out_shape=out_shape, in_specs=[hbm] * 3, out_spec...  1.92 us

profile of v4, /device:TPU:1, one launch (start us, length us, event | category | flops | bytes accessed | tf_op | source)
XLA Modules:
  0.0 93.5 jit_solution(8152134378595440915)
XLA Ops:
  0.6 91.0 %shard_map.67 = (bf16[96,256]{1,0:T(8,128)(2,1)}, bf16[768,256]{1,0:T(8,128)(2,1)}, f32[96,768]{1,0:T(8,128)}) custom-call(bf16[96,256]{1,0:T(8,128)(2,1)} %bitcast.5, bf16[96,256]{1,0:T(8,128)(2,1)} %bitcast.6, bf16[768,256]{1,0:T(8,128)(2,1)} %win.1, bf16[256,768]{1,0:T(8,128)(2,1)} %wout.1), custom_call_target="tpu_custom_call" | custom-call | flops 3600000000 | bytes 4000000 | tf_op jit(solution)/shard_map/pallas_call | solution.py:407
  91.6 1.9 %shard_map.68 = (bf16[96,256]{1,0:T(8,128)(2,1)}, bf16[768,256]{1,0:T(8,128)(2,1)}, f32[96,768]{1,0:T(8,128)}) custom-call(bf16[96,256]{1,0:T(8,128)(2,1)} %get-tuple-element.9.refs_0_, bf16[768,256]{1,0:T(8,128)(2,1)} %get-tuple-element.10.refs_1_, f32[96,768]{1,0:T(8,128)} %get-tuple-element.11.refs_2_), custom_call_target="tpu_custom_call" | custom-call | tf_op jit(solution)/shard_map/pallas_call | solution.py:450

commit v5 on v4

--- a/solution.py
+++ b/solution.py
@@ -14,41 +14,47 @@
 NH = 2
 CH = 256 // NH
 NP = 6
-KINDS = 16
-ZT = 1
-SLOTS = 156
-TOGETHER = {"ah": 2, "dx": 2, "sq": 1}
+KINDS = 17
+ZT = 2
+SLOTS = 184
+TOGETHER = {"ah": 2, "dx": 2, "sq": 1, "g3": 1}
 LATE = (2, 3, 4, 5)
 
 SCHEDULE = [
-    ("start",), ("wstart", 0), ("z", 0, 0, 0, 1, 0), ("wstart", 1), ("z", 0, 0, 1, 1, 0), ("z", 0, 1, 0, 1, 0),
-    ("z", 0, 1, 1, 1, 0), ("hs", 0, 0), ("z", 0, 0, 0, 2, 0), ("hs", 1, 0), ("z", 0, 1, 1, 2, 0),
-    ("z", 0, 0, 1, 2, 0), ("z", 1, 0, 0, 1, 0), ("z", 0, 0, 0, 3, 0), ("z", 1, 1, 1, 1, 0), ("z", 0, 1, 0, 2, 0),
-    ("z", 1, 1, 0, 1, 0), ("wf", 0, 0), ("z", 0, 1, 1, 3, 0), ("z", 1, 0, 0, 2, 0), ("z", 1, 0, 1, 1, 0),
-    ("z", 0, 0, 0, 4, 0), ("wf", 1, 0), ("z", 1, 1, 1, 2, 0), ("z", 0, 1, 0, 3, 0), ("z", 0, 0, 1, 3, 0),
-    ("wf", 0, 1), ("z", 0, 1, 1, 4, 0), ("A", 1, 0, 0), ("A", 3, 0, 0), ("A", 0, 1, 0), ("B", 1, 0, 0),
-    ("z", 1, 0, 1, 2, 0), ("z", 1, 1, 0, 2, 0), ("B", 3, 0, 0), ("z", 1, 0, 0, 3, 0), ("B", 0, 1, 0), ("wf", 1, 1),
-    ("A", 1, 1, 0), ("z", 1, 1, 1, 3, 0), ("A", 3, 1, 0), ("B", 1, 1, 0), ("B2", 3, 0, 0), ("z", 1, 0, 1, 3, 0),
-    ("B2", 1, 0, 0), ("B", 3, 1, 0), ("B2", 0, 1, 0), ("z", 1, 0, 0, 4, 0), ("A", 2, 0, 0), ("z", 1, 1, 0, 3, 0),
-    ("z", 1, 1, 1, 4, 0), ("A", 2, 0, 1), ("B2", 1, 1, 0), ("B", 2, 0, 0), ("A", 3, 0, 1), ("B", 2, 0, 1),
-    ("A", 1, 0, 1), ("B", 3, 0, 1), ("A", 1, 1, 1), ("B2", 3, 1, 0), ("B", 1, 0, 1), ("C", 3, 0, 0), ("A", 0, 1, 1),
-    ("A", 2, 1, 0), ("B2", 2, 0, 0), ("A", 2, 1, 1), ("B2", 2, 0, 1), ("B", 2, 1, 0), ("A", 0, 0, 1), ("B", 2, 1, 1),
-    ("B2", 3, 0, 1), ("B2", 1, 0, 1), ("B", 1, 1, 1), ("A", 3, 1, 1), ("C", 1, 0, 0), ("C", 2, 0, 0), ("B", 3, 1, 1),
-    ("B2", 2, 1, 0), ("B2", 2, 1, 1), ("C", 2, 0, 1), ("C", 3, 0, 1), ("B", 0, 1, 1), ("D", 3, 0, 0), ("B", 0, 0, 1),
-    ("C", 1, 0, 1), ("B2", 1, 1, 1), ("A", 0, 0, 0), ("B2", 3, 1, 1), ("E", 3, 0, 0), ("C", 2, 1, 0), ("D", 1, 0, 0),
-    ("D", 2, 0, 0), ("C", 2, 1, 1), ("E", 1, 0, 0), ("B2", 0, 1, 1), ("D", 2, 0, 1), ("E", 2, 0, 0), ("B2", 0, 0, 1),
-    ("C", 1, 1, 0), ("D", 3, 0, 1), ("E", 2, 0, 1), ("dw", 2, 0), ("B", 0, 0, 0), ("C", 3, 1, 0), ("E", 3, 0, 1),
-    ("D", 1, 0, 1), ("C", 3, 1, 1), ("C", 1, 1, 1), ("dw", 3, 0), ("E", 1, 0, 1), ("dw", 1, 0), ("D", 2, 1, 1),
-    ("C", 0, 1, 1), ("D", 2, 1, 0), ("C", 0, 0, 1), ("E", 2, 1, 1), ("B2", 0, 0, 0), ("E", 2, 1, 0), ("dw", 2, 1),
-    ("C", 0, 1, 0), ("D", 1, 1, 0), ("add", 0, 1), ("D", 3, 1, 0), ("D", 3, 1, 1), ("add", 0, 0), ("D", 1, 1, 1),
-    ("E", 1, 1, 0), ("E", 3, 1, 0), ("E", 3, 1, 1), ("D", 0, 1, 1), ("dw", 3, 1), ("E", 1, 1, 1), ("D", 0, 0, 1),
-    ("dw", 1, 1), ("C", 0, 0, 0), ("E", 0, 1, 1), ("E", 0, 0, 1), ("dx", 1), ("D", 0, 1, 0), ("add", 1, 0),
-    ("add", 1, 1), ("E", 0, 1, 0), ("dw", 0, 1), ("D", 0, 0, 0), ("E", 0, 0, 0), ("dw", 0, 0), ("own", 0), ("own", 1),
-    ("sq",), ("g", 5), ("g", 0), ("g", 1), ("g", 3), ("sq2",), ("g2", 5), ("g", 4), ("dx", 0), ("g", 2), ("ga", 5, 0),
-    ("ga", 5, 1), ("g2", 0), ("ga", 0, 0), ("ga", 0, 1), ("ga", 1, 1), ("g2", 1), ("dxs", 1), ("ga", 1, 0),
-    ("ga", 4, 0), ("g2", 4), ("ga", 4, 1), ("ga", 3, 0), ("ga", 3, 1), ("go", 5), ("g2", 3), ("ga", 2, 0),
-    ("ga", 2, 1), ("go", 0), ("g2", 2), ("go", 1), ("go", 4), ("go", 3), ("go", 2), ("gf", 0), ("gf", 5), ("gf", 1),
-    ("gf", 4), ("gf", 3), ("dxs", 0), ("dxf",), ("gf", 2),
+    ("start",), ("wstart", 0), ("z", 0, 0, 1, 1, 0), ("z", 0, 0, 0, 1, 0), ("z", 0, 1, 1, 1, 0), ("z", 0, 0, 1, 1, 1),
+    ("z", 0, 0, 0, 1, 1), ("z", 0, 1, 1, 1, 1), ("z", 0, 1, 0, 1, 1), ("wstart", 1), ("z", 0, 1, 0, 1, 0),
+    ("hs", 0, 0), ("hs", 0, 1), ("z", 0, 0, 0, 2, 0), ("hs", 1, 0), ("z", 0, 1, 1, 2, 0), ("z", 0, 0, 0, 2, 1),
+    ("hs", 1, 1), ("z", 0, 1, 1, 2, 1), ("z", 0, 0, 1, 2, 1), ("z", 0, 0, 1, 2, 0), ("z", 1, 0, 0, 1, 0),
+    ("z", 1, 0, 0, 1, 1), ("z", 0, 1, 0, 2, 0), ("z", 1, 1, 1, 1, 0), ("z", 0, 1, 0, 2, 1), ("z", 0, 1, 1, 3, 0),
+    ("z", 0, 0, 0, 3, 0), ("z", 1, 1, 1, 1, 1), ("z", 0, 0, 0, 3, 1), ("wf", 0, 1), ("z", 0, 1, 1, 3, 1),
+    ("z", 1, 1, 0, 1, 0), ("z", 1, 0, 1, 1, 0), ("z", 1, 0, 0, 2, 0), ("z", 1, 0, 1, 1, 1), ("z", 0, 0, 1, 3, 0),
+    ("z", 1, 0, 0, 2, 1), ("z", 0, 1, 0, 3, 0), ("z", 1, 1, 0, 1, 1), ("wf", 0, 0), ("z", 1, 1, 1, 2, 0),
+    ("z", 1, 1, 1, 2, 1), ("z", 0, 0, 0, 4, 1), ("z", 0, 0, 0, 4, 0), ("z", 0, 1, 1, 4, 0), ("z", 0, 0, 1, 3, 1),
+    ("z", 0, 1, 1, 4, 1), ("z", 0, 1, 0, 3, 1), ("A", 3, 0, 0), ("wf", 1, 0), ("z", 1, 1, 0, 2, 0),
+    ("z", 1, 0, 1, 2, 0), ("A", 1, 0, 0), ("z", 1, 0, 0, 3, 0), ("z", 1, 0, 1, 2, 1), ("B", 3, 0, 0),
+    ("z", 1, 1, 0, 2, 1), ("z", 1, 0, 0, 3, 1), ("B", 1, 0, 0), ("z", 1, 1, 1, 3, 0), ("A", 0, 0, 0),
+    ("z", 1, 1, 1, 3, 1), ("B", 0, 0, 0), ("A", 3, 1, 0), ("wf", 1, 1), ("A", 1, 1, 0), ("B2", 3, 0, 0),
+    ("z", 1, 1, 0, 3, 0), ("z", 1, 0, 1, 3, 1), ("z", 1, 0, 1, 3, 0), ("z", 1, 0, 0, 4, 0), ("B", 3, 1, 0),
+    ("z", 1, 1, 1, 4, 0), ("z", 1, 0, 0, 4, 1), ("B", 1, 1, 0), ("z", 1, 1, 0, 3, 1), ("z", 1, 1, 1, 4, 1),
+    ("A", 3, 1, 1), ("A", 1, 0, 1), ("B2", 1, 0, 0), ("A", 3, 0, 1), ("B", 3, 1, 1), ("B", 1, 0, 1), ("B", 3, 0, 1),
+    ("A", 2, 0, 1), ("A", 2, 0, 0), ("B2", 3, 1, 0), ("B", 2, 0, 1), ("B2", 1, 1, 0), ("B", 2, 0, 0), ("C", 3, 0, 0),
+    ("B2", 3, 1, 1), ("A", 0, 1, 0), ("B2", 1, 0, 1), ("C", 1, 0, 0), ("A", 1, 1, 1), ("B2", 3, 0, 1), ("A", 2, 1, 0),
+    ("A", 2, 1, 1), ("B2", 2, 0, 1), ("B", 2, 1, 0), ("B", 2, 1, 1), ("B2", 2, 0, 0), ("A", 0, 1, 1), ("C", 3, 1, 0),
+    ("C", 3, 1, 1), ("D", 3, 0, 0), ("C", 1, 0, 1), ("B", 1, 1, 1), ("B2", 2, 1, 0), ("B2", 2, 1, 1), ("C", 2, 0, 1),
+    ("A", 0, 0, 1), ("B", 0, 1, 1), ("C", 2, 0, 0), ("D", 1, 0, 0), ("B", 0, 0, 1), ("C", 3, 0, 1), ("D", 3, 1, 0),
+    ("B2", 1, 1, 1), ("D", 3, 1, 1), ("D", 1, 0, 1), ("C", 2, 1, 0), ("E", 3, 1, 0), ("E", 1, 0, 0), ("C", 2, 1, 1),
+    ("E", 3, 1, 1), ("B2", 0, 1, 1), ("E", 1, 0, 1), ("dw", 1, 0), ("dw", 3, 1), ("B2", 0, 0, 1), ("D", 2, 0, 1),
+    ("B2", 0, 0, 0), ("D", 2, 0, 0), ("B", 0, 1, 0), ("C", 1, 1, 0), ("E", 2, 0, 1), ("E", 2, 0, 0), ("dw", 2, 0),
+    ("C", 1, 1, 1), ("D", 2, 1, 0), ("D", 2, 1, 1), ("C", 0, 1, 1), ("E", 2, 1, 0), ("D", 3, 0, 1), ("E", 3, 0, 0),
+    ("C", 0, 0, 1), ("E", 2, 1, 1), ("dw", 2, 1), ("E", 3, 0, 1), ("B2", 0, 1, 0), ("C", 0, 0, 0), ("dw", 3, 0),
+    ("D", 1, 1, 0), ("add", 0, 0), ("D", 1, 1, 1), ("add", 0, 1), ("E", 1, 1, 1), ("E", 1, 1, 0), ("D", 0, 1, 1),
+    ("dw", 1, 1), ("D", 0, 0, 1), ("C", 0, 1, 0), ("E", 0, 1, 1), ("E", 0, 0, 1), ("dx", 1), ("add", 1, 1),
+    ("D", 0, 0, 0), ("add", 1, 0), ("D", 0, 1, 0), ("E", 0, 1, 0), ("E", 0, 0, 0), ("dw", 0, 0), ("own", 0),
+    ("dw", 0, 1), ("own", 1), ("sq",), ("g", 4), ("g", 0), ("g", 5), ("g", 3), ("g2", 3), ("g", 2), ("g2", 4),
+    ("dx", 0), ("g", 1), ("sq2",), ("ga", 4, 1), ("ga", 4, 0), ("ga", 5, 0), ("ga", 5, 1), ("g2", 5), ("ga", 3, 0),
+    ("dxs", 1), ("ga", 3, 1), ("g2", 2), ("ga", 2, 1), ("g2", 1), ("ga", 2, 0), ("ga", 1, 1), ("go", 4), ("ga", 1, 0),
+    ("go", 5), ("go", 3), ("go", 2), ("go", 1), ("gx", 0), ("gf", 5), ("gf", 4), ("dxs", 0), ("gf", 2), ("gf", 3),
+    ("dxf",), ("gf", 0), ("gf", 1),
 ]
 
 
@@ -72,7 +78,7 @@
     x_in, g_in, win, wout, dx_out, dw_out, gram_out,
     xg, wi, wo, psend, pown, crecv, ysend, yrecv, y2send, y2recv, ht,
     dxacc, dxo, dxs, dxr, dxh, dxhr, dwf, dwf0, dws, dwr,
-    gbuf, gsend, grecv, ghs, ghr, sqs, sqr, l_sem, s_all, r_all,
+    gbuf, gsend, grecv, ghs, ghr, gys, gyr, g3s, g3r, sqs, sqr, l_sem, s_all, r_all,
 ):
     gx = lax.axis_index("gx")
     gy = lax.axis_index("gy")
@@ -312,8 +318,20 @@
     def do_g(p):
         ws = scaled["w"]
         gbuf[p] = dot(ws, ws[p * width : (p + 1) * width], 1, 1).reshape(2, 4, 96, width)
+        if p == 0:
+            gys[...] = gbuf[p, 1 - hi].astype(BF)
+            send(gys, gyr, ("gy",), h_dev)
+            return
         put_g(p, 0, gbuf[p, 0, x2], xp)
         put_g(p, 1, gbuf[p, 1, x2], xm)
+
+    def do_gx(p):
+        arrived(gyr, ("gy",))
+        total = gbuf[p, hi] + gyr[...].astype(F32)
+        gbuf[p, hi] = total
+        g3s[...] = total.astype(BF)
+        for k, to in ((2, x2), (1, x1), (3, x3)):
+            send(g3s.at[to], g3r.at[k - 1], ("g3", k), {"gx": hi * 4 + to})
 
     def do_g2(p):
         put_g(p, 2, gbuf[p, 1, x1], xp)
@@ -339,8 +357,15 @@
                 sq = sq + sqr[k - 1]
             scaled["factor"] = DOWN / (jnp.sqrt(sq[:1, :1]) + 1e-07)
         factor = scaled["factor"]
-        arrived(ghr.at[p], ("gh", p))
-        val = (gbuf[p, hi, xx] + ghr[p].astype(F32)) * factor * factor * 768.0
+        val = gbuf[p, hi, xx]
+        if p == 0:
+            arrived(g3r, ("g3", 1))
+            for k in range(3):
+                val = val + g3r[k].astype(F32)
+        else:
+            arrived(ghr.at[p], ("gh", p))
+            val = val + ghr[p].astype(F32)
+        val = val * factor * factor * 768.0
         gram_out[:, p * width : (p + 1) * width] = val
 
     def do_dxs(r):
@@ -361,7 +386,7 @@
     steps = {
         "start": do_start, "wstart": do_wstart, "hs": do_hs, "z": do_z, "wf": do_wf,
         "A": do_a, "B": do_b, "B2": do_b2, "C": do_c, "D": do_d, "E": do_e, "dw": do_dw, "add": do_add, "own": do_own,
-        "sq": do_sq, "sq2": do_sq2, "g": do_g, "g2": do_g2, "ga": do_ga, "go": do_go, "gf": do_gf,
+        "sq": do_sq, "sq2": do_sq2, "g": do_g, "gx": do_gx, "g2": do_g2, "ga": do_ga, "go": do_go, "gf": do_gf,
         "dx": do_dx, "dxs": do_dxs, "dxf": do_dxf,
     }
     for step in SCHEDULE:
@@ -370,7 +395,7 @@
     totals = {
         "h": xg.at[:, 0, :96, :], "z": xg.at[:, :, :672, :], "w0": wi.at[:3], "w1": wo.at[:3],
         "c": crecv, "y": yrecv, "y2": y2recv, "ah": ht.at[:, : 3 * CH // 8, :], "ac": ht.at[:, : CH // 2, :],
-        "dw": dwr, "dx": dxr, "sq": sqr, "g": grecv, "gh": ghr, "dxh": dxhr,
+        "dw": dwr, "dx": dxr, "sq": sqr, "g": grecv.at[1:], "gh": ghr.at[1:], "gy": gyr, "g3": g3r, "dxh": dxhr,
     }
     for kind, ref in totals.items():
         k = kinds[kind]
@@ -436,6 +461,10 @@
             pltpu.VMEM((NP, 6, 96, width), BF),
             pltpu.VMEM((NP, 96, width), BF),
             pltpu.VMEM((NP, 96, width), BF),
+            pltpu.VMEM((4, 96, width), BF),
+            pltpu.VMEM((4, 96, width), BF),
+            pltpu.VMEM((4, 96, width), BF),
+            pltpu.VMEM((3, 96, width), BF),
             pltpu.VMEM((8, 128), F32),
             pltpu.VMEM((7, 8, 128), F32),
             dma((4,)), dma((KINDS,)), dma((SLOTS,)),

time: 94.1 us -> 92.4 us (0.982)
  Pallas kernels: 92.9 us -> 91.4 us
    pallas_call x1, Pallas kernels: 91 us -> 89.5 us  [body(): pl.pallas_call(kernel, out_shape=out_shape, in_specs=[hbm] * 4, out_specs...]
where the time goes in v5:
time: 92.4 us; the launch traced here: 92 us
  Pallas kernels  91.4 us (99%)
    pallas_call x1, Pallas kernels, body(): pl.pallas_call(kernel, out_shape=out_shape, in_specs=[hbm] * 4, out_specs...  89.5 us
    pallas_call x1, Pallas kernels, body(): pl.pallas_call(hand_on, out_shape=out_shape, in_specs=[hbm] * 3, out_spec...  1.92 us

profile of v5, /device:TPU:1, one launch (start us, length us, event | category | flops | bytes accessed | tf_op | source)
XLA Modules:
  0.0 92.0 jit_solution(13806267547255967921)
XLA Ops:
  0.6 89.5 %shard_map.67 = (bf16[96,256]{1,0:T(8,128)(2,1)}, bf16[768,256]{1,0:T(8,128)(2,1)}, f32[96,768]{1,0:T(8,128)}) custom-call(bf16[96,256]{1,0:T(8,128)(2,1)} %bitcast.5, bf16[96,256]{1,0:T(8,128)(2,1)} %bitcast.6, bf16[768,256]{1,0:T(8,128)(2,1)} %win.1, bf16[256,768]{1,0:T(8,128)(2,1)} %wout.1), custom_call_target="tpu_custom_call" | custom-call | flops 3600000000 | bytes 4000000 | tf_op jit(solution)/shard_map/pallas_call | solution.py:432
  90.1 1.9 %shard_map.68 = (bf16[96,256]{1,0:T(8,128)(2,1)}, bf16[768,256]{1,0:T(8,128)(2,1)}, f32[96,768]{1,0:T(8,128)}) custom-call(bf16[96,256]{1,0:T(8,128)(2,1)} %get-tuple-element.9.refs_0_, bf16[768,256]{1,0:T(8,128)(2,1)} %get-tuple-element.10.refs_1_, f32[96,768]{1,0:T(8,128)} %get-tuple-element.11.refs_2_), custom_call_target="tpu_custom_call" | custom-call | tf_op jit(solution)/shard_map/pallas_call | solution.py:479

commit v6 on v5

--- a/solution.py
+++ b/solution.py
@@ -21,40 +21,39 @@
 LATE = (2, 3, 4, 5)
 
 SCHEDULE = [
-    ("start",), ("wstart", 0), ("z", 0, 0, 1, 1, 0), ("z", 0, 0, 0, 1, 0), ("z", 0, 1, 1, 1, 0), ("z", 0, 0, 1, 1, 1),
-    ("z", 0, 0, 0, 1, 1), ("z", 0, 1, 1, 1, 1), ("z", 0, 1, 0, 1, 1), ("wstart", 1), ("z", 0, 1, 0, 1, 0),
-    ("hs", 0, 0), ("hs", 0, 1), ("z", 0, 0, 0, 2, 0), ("hs", 1, 0), ("z", 0, 1, 1, 2, 0), ("z", 0, 0, 0, 2, 1),
-    ("hs", 1, 1), ("z", 0, 1, 1, 2, 1), ("z", 0, 0, 1, 2, 1), ("z", 0, 0, 1, 2, 0), ("z", 1, 0, 0, 1, 0),
-    ("z", 1, 0, 0, 1, 1), ("z", 0, 1, 0, 2, 0), ("z", 1, 1, 1, 1, 0), ("z", 0, 1, 0, 2, 1), ("z", 0, 1, 1, 3, 0),
-    ("z", 0, 0, 0, 3, 0), ("z", 1, 1, 1, 1, 1), ("z", 0, 0, 0, 3, 1), ("wf", 0, 1), ("z", 0, 1, 1, 3, 1),
-    ("z", 1, 1, 0, 1, 0), ("z", 1, 0, 1, 1, 0), ("z", 1, 0, 0, 2, 0), ("z", 1, 0, 1, 1, 1), ("z", 0, 0, 1, 3, 0),
-    ("z", 1, 0, 0, 2, 1), ("z", 0, 1, 0, 3, 0), ("z", 1, 1, 0, 1, 1), ("wf", 0, 0), ("z", 1, 1, 1, 2, 0),
-    ("z", 1, 1, 1, 2, 1), ("z", 0, 0, 0, 4, 1), ("z", 0, 0, 0, 4, 0), ("z", 0, 1, 1, 4, 0), ("z", 0, 0, 1, 3, 1),
-    ("z", 0, 1, 1, 4, 1), ("z", 0, 1, 0, 3, 1), ("A", 3, 0, 0), ("wf", 1, 0), ("z", 1, 1, 0, 2, 0),
-    ("z", 1, 0, 1, 2, 0), ("A", 1, 0, 0), ("z", 1, 0, 0, 3, 0), ("z", 1, 0, 1, 2, 1), ("B", 3, 0, 0),
-    ("z", 1, 1, 0, 2, 1), ("z", 1, 0, 0, 3, 1), ("B", 1, 0, 0), ("z", 1, 1, 1, 3, 0), ("A", 0, 0, 0),
-    ("z", 1, 1, 1, 3, 1), ("B", 0, 0, 0), ("A", 3, 1, 0), ("wf", 1, 1), ("A", 1, 1, 0), ("B2", 3, 0, 0),
-    ("z", 1, 1, 0, 3, 0), ("z", 1, 0, 1, 3, 1), ("z", 1, 0, 1, 3, 0), ("z", 1, 0, 0, 4, 0), ("B", 3, 1, 0),
-    ("z", 1, 1, 1, 4, 0), ("z", 1, 0, 0, 4, 1), ("B", 1, 1, 0), ("z", 1, 1, 0, 3, 1), ("z", 1, 1, 1, 4, 1),
-    ("A", 3, 1, 1), ("A", 1, 0, 1), ("B2", 1, 0, 0), ("A", 3, 0, 1), ("B", 3, 1, 1), ("B", 1, 0, 1), ("B", 3, 0, 1),
-    ("A", 2, 0, 1), ("A", 2, 0, 0), ("B2", 3, 1, 0), ("B", 2, 0, 1), ("B2", 1, 1, 0), ("B", 2, 0, 0), ("C", 3, 0, 0),
-    ("B2", 3, 1, 1), ("A", 0, 1, 0), ("B2", 1, 0, 1), ("C", 1, 0, 0), ("A", 1, 1, 1), ("B2", 3, 0, 1), ("A", 2, 1, 0),
-    ("A", 2, 1, 1), ("B2", 2, 0, 1), ("B", 2, 1, 0), ("B", 2, 1, 1), ("B2", 2, 0, 0), ("A", 0, 1, 1), ("C", 3, 1, 0),
-    ("C", 3, 1, 1), ("D", 3, 0, 0), ("C", 1, 0, 1), ("B", 1, 1, 1), ("B2", 2, 1, 0), ("B2", 2, 1, 1), ("C", 2, 0, 1),
-    ("A", 0, 0, 1), ("B", 0, 1, 1), ("C", 2, 0, 0), ("D", 1, 0, 0), ("B", 0, 0, 1), ("C", 3, 0, 1), ("D", 3, 1, 0),
-    ("B2", 1, 1, 1), ("D", 3, 1, 1), ("D", 1, 0, 1), ("C", 2, 1, 0), ("E", 3, 1, 0), ("E", 1, 0, 0), ("C", 2, 1, 1),
-    ("E", 3, 1, 1), ("B2", 0, 1, 1), ("E", 1, 0, 1), ("dw", 1, 0), ("dw", 3, 1), ("B2", 0, 0, 1), ("D", 2, 0, 1),
-    ("B2", 0, 0, 0), ("D", 2, 0, 0), ("B", 0, 1, 0), ("C", 1, 1, 0), ("E", 2, 0, 1), ("E", 2, 0, 0), ("dw", 2, 0),
-    ("C", 1, 1, 1), ("D", 2, 1, 0), ("D", 2, 1, 1), ("C", 0, 1, 1), ("E", 2, 1, 0), ("D", 3, 0, 1), ("E", 3, 0, 0),
-    ("C", 0, 0, 1), ("E", 2, 1, 1), ("dw", 2, 1), ("E", 3, 0, 1), ("B2", 0, 1, 0), ("C", 0, 0, 0), ("dw", 3, 0),
-    ("D", 1, 1, 0), ("add", 0, 0), ("D", 1, 1, 1), ("add", 0, 1), ("E", 1, 1, 1), ("E", 1, 1, 0), ("D", 0, 1, 1),
-    ("dw", 1, 1), ("D", 0, 0, 1), ("C", 0, 1, 0), ("E", 0, 1, 1), ("E", 0, 0, 1), ("dx", 1), ("add", 1, 1),
-    ("D", 0, 0, 0), ("add", 1, 0), ("D", 0, 1, 0), ("E", 0, 1, 0), ("E", 0, 0, 0), ("dw", 0, 0), ("own", 0),
-    ("dw", 0, 1), ("own", 1), ("sq",), ("g", 4), ("g", 0), ("g", 5), ("g", 3), ("g2", 3), ("g", 2), ("g2", 4),
-    ("dx", 0), ("g", 1), ("sq2",), ("ga", 4, 1), ("ga", 4, 0), ("ga", 5, 0), ("ga", 5, 1), ("g2", 5), ("ga", 3, 0),
-    ("dxs", 1), ("ga", 3, 1), ("g2", 2), ("ga", 2, 1), ("g2", 1), ("ga", 2, 0), ("ga", 1, 1), ("go", 4), ("ga", 1, 0),
-    ("go", 5), ("go", 3), ("go", 2), ("go", 1), ("gx", 0), ("gf", 5), ("gf", 4), ("dxs", 0), ("gf", 2), ("gf", 3),
-    ("dxf",), ("gf", 0), ("gf", 1),
+    ("start",), ("wstart", 0), ("z", 0, 0, 1, 1, 0), ("z", 0, 0, 0, 1, 1), ("z", 0, 0, 0, 1, 0), ("z", 0, 1, 1, 1, 0),
+    ("z", 0, 1, 0, 1, 0), ("z", 0, 1, 1, 1, 1), ("hs", 0, 0), ("z", 0, 0, 1, 1, 1), ("z", 0, 1, 0, 1, 1),
+    ("hs", 0, 1), ("hs", 1, 0), ("z", 0, 0, 0, 2, 0), ("hs", 1, 1), ("wstart", 1), ("z", 0, 1, 1, 2, 1),
+    ("z", 0, 1, 0, 2, 0), ("z", 0, 0, 0, 2, 1), ("z", 0, 0, 1, 2, 0), ("z", 0, 1, 1, 2, 0), ("z", 1, 0, 0, 1, 0),
+    ("z", 1, 0, 1, 1, 0), ("z", 1, 0, 0, 1, 1), ("z", 1, 1, 1, 1, 0), ("z", 1, 1, 1, 1, 1), ("z", 0, 0, 1, 2, 1),
+    ("z", 1, 1, 0, 1, 0), ("z", 0, 0, 0, 3, 0), ("wf", 0, 0), ("z", 0, 1, 1, 3, 1), ("z", 1, 1, 0, 1, 1),
+    ("z", 1, 0, 1, 1, 1), ("z", 0, 1, 0, 2, 1), ("z", 0, 0, 1, 3, 0), ("z", 0, 1, 1, 3, 0), ("z", 0, 0, 0, 3, 1),
+    ("wf", 0, 1), ("z", 1, 0, 0, 2, 0), ("z", 1, 0, 1, 2, 0), ("z", 1, 0, 0, 2, 1), ("z", 1, 1, 1, 2, 0),
+    ("z", 1, 1, 1, 2, 1), ("z", 0, 1, 0, 3, 0), ("z", 0, 0, 0, 4, 0), ("z", 1, 1, 0, 2, 1), ("z", 0, 0, 1, 3, 1),
+    ("z", 1, 0, 1, 2, 1), ("z", 0, 1, 1, 4, 1), ("z", 1, 1, 0, 2, 0), ("z", 0, 1, 1, 4, 0), ("z", 0, 1, 0, 3, 1),
+    ("z", 0, 0, 0, 4, 1), ("A", 1, 0, 0), ("A", 3, 0, 0), ("z", 1, 0, 0, 3, 0), ("z", 1, 1, 1, 3, 0),
+    ("z", 1, 0, 0, 3, 1), ("B", 1, 0, 0), ("z", 1, 1, 1, 3, 1), ("A", 0, 0, 0), ("B", 3, 0, 0), ("wf", 1, 1),
+    ("A", 1, 1, 0), ("z", 1, 0, 1, 3, 1), ("z", 1, 0, 1, 3, 0), ("B", 0, 0, 0), ("z", 1, 1, 0, 3, 1), ("wf", 1, 0),
+    ("A", 3, 1, 0), ("B", 1, 1, 0), ("z", 1, 0, 0, 4, 0), ("B", 3, 1, 0), ("z", 1, 1, 0, 3, 0), ("z", 1, 1, 1, 4, 0),
+    ("z", 1, 0, 0, 4, 1), ("z", 1, 1, 1, 4, 1), ("A", 3, 0, 1), ("B2", 1, 0, 0), ("A", 1, 0, 1), ("B2", 3, 0, 0),
+    ("B", 3, 0, 1), ("A", 2, 0, 1), ("B", 1, 0, 1), ("A", 2, 0, 0), ("B2", 1, 1, 0), ("A", 1, 1, 1), ("B", 2, 0, 1),
+    ("A", 3, 1, 1), ("B", 2, 0, 0), ("B2", 3, 1, 0), ("A", 0, 1, 1), ("C", 1, 0, 0), ("B2", 3, 0, 1), ("B", 3, 1, 1),
+    ("B2", 1, 0, 1), ("A", 2, 1, 1), ("A", 2, 1, 0), ("B2", 2, 0, 1), ("B", 2, 1, 1), ("B", 2, 1, 0), ("B2", 2, 0, 0),
+    ("B", 1, 1, 1), ("C", 3, 0, 0), ("B", 0, 1, 1), ("B2", 3, 1, 1), ("C", 3, 0, 1), ("B2", 2, 1, 1), ("B2", 2, 1, 0),
+    ("A", 0, 0, 1), ("C", 2, 0, 1), ("C", 2, 0, 0), ("B", 0, 0, 1), ("A", 0, 1, 0), ("C", 1, 0, 1), ("B2", 0, 1, 1),
+    ("B2", 1, 1, 1), ("D", 3, 0, 0), ("D", 1, 0, 0), ("C", 2, 1, 1), ("C", 2, 1, 0), ("C", 3, 1, 1), ("B", 0, 1, 0),
+    ("D", 2, 0, 1), ("B2", 0, 0, 1), ("C", 3, 1, 0), ("D", 2, 0, 0), ("C", 1, 1, 0), ("E", 3, 0, 0), ("E", 2, 0, 1),
+    ("D", 3, 0, 1), ("E", 2, 0, 0), ("dw", 2, 0), ("C", 1, 1, 1), ("D", 1, 0, 1), ("B2", 0, 0, 0), ("E", 3, 0, 1),
+    ("dw", 3, 0), ("E", 1, 0, 0), ("E", 1, 0, 1), ("dw", 1, 0), ("D", 2, 1, 1), ("C", 0, 1, 1), ("D", 2, 1, 0),
+    ("D", 3, 1, 1), ("C", 0, 0, 1), ("E", 2, 1, 1), ("E", 2, 1, 0), ("dw", 2, 1), ("B2", 0, 1, 0), ("E", 3, 1, 1),
+    ("D", 3, 1, 0), ("add", 0, 1), ("add", 0, 0), ("D", 1, 1, 1), ("E", 3, 1, 0), ("C", 0, 0, 0), ("D", 1, 1, 0),
+    ("E", 1, 1, 1), ("dw", 3, 1), ("D", 0, 1, 1), ("E", 1, 1, 0), ("dw", 1, 1), ("D", 0, 0, 1), ("C", 0, 1, 0),
+    ("E", 0, 1, 1), ("E", 0, 0, 1), ("dx", 1), ("add", 1, 0), ("add", 1, 1), ("D", 0, 0, 0), ("D", 0, 1, 0),
+    ("E", 0, 0, 0), ("dw", 0, 0), ("E", 0, 1, 0), ("own", 0), ("dw", 0, 1), ("own", 1), ("sq",), ("g", 4), ("g", 0),
+    ("g", 5), ("g", 3), ("g", 2), ("g2", 4), ("g", 1), ("dx", 0), ("ga", 4, 0), ("ga", 4, 1), ("g2", 5), ("ga", 5, 0),
+    ("ga", 5, 1), ("g2", 2), ("dxs", 1), ("ga", 2, 0), ("ga", 2, 1), ("ga", 3, 1), ("g2", 3), ("ga", 3, 0), ("g2", 1),
+    ("sq2",), ("ga", 1, 1), ("ga", 1, 0), ("go", 4), ("go", 5), ("go", 2), ("gx", 0), ("go", 3), ("go", 1), ("gf", 2),
+    ("gf", 5), ("gf", 3), ("gf", 4), ("gf", 0), ("dxs", 0), ("dxf",), ("gf", 1),
 ]
 
 

time: 92.4 us -> 93.8 us (1.015)
  no operation moved by 1% of the time
where the time goes in v6:
time: 93.8 us; the launch traced here: 92.5 us
  Pallas kernels  91.9 us (98%)
    pallas_call x1, Pallas kernels, body(): pl.pallas_call(kernel, out_shape=out_shape, in_specs=[hbm] * 4, out_specs...  90 us
    pallas_call x1, Pallas kernels, body(): pl.pallas_call(hand_on, out_shape=out_shape, in_specs=[hbm] * 3, out_spec...  1.92 us

profile of v6, /device:TPU:1, one launch (start us, length us, event | category | flops | bytes accessed | tf_op | source)
XLA Modules:
  0.0 92.5 jit_solution(1260459056142407935)
XLA Ops:
  0.6 90.0 %shard_map.67 = (bf16[96,256]{1,0:T(8,128)(2,1)}, bf16[768,256]{1,0:T(8,128)(2,1)}, f32[96,768]{1,0:T(8,128)}) custom-call(bf16[96,256]{1,0:T(8,128)(2,1)} %bitcast.5, bf16[96,256]{1,0:T(8,128)(2,1)} %bitcast.6, bf16[768,256]{1,0:T(8,128)(2,1)} %win.1, bf16[256,768]{1,0:T(8,128)(2,1)} %wout.1), custom_call_target="tpu_custom_call" | custom-call | flops 3600000000 | bytes 4000000 | tf_op jit(solution)/shard_map/pallas_call | solution.py:431
  90.6 1.9 %shard_map.68 = (bf16[96,256]{1,0:T(8,128)(2,1)}, bf16[768,256]{1,0:T(8,128)(2,1)}, f32[96,768]{1,0:T(8,128)}) custom-call(bf16[96,256]{1,0:T(8,128)(2,1)} %get-tuple-element.9.refs_0_, bf16[768,256]{1,0:T(8,128)(2,1)} %get-tuple-element.10.refs_1_, f32[96,768]{1,0:T(8,128)} %get-tuple-element.11.refs_2_), custom_call_target="tpu_custom_call" | custom-call | tf_op jit(solution)/shard_map/pallas_call | solution.py:478
